TPU v7x, 128 devices: a whole 4x4x4 slice. The times are simulated.
128 devices in a mesh: ctx: 64 (over z, y_lo, x, core), tp: 2 (over y_hi).
Axes of the slice: x: 4, y: 4 (y_hi: 2, y_lo: 2; y = y_hi * 2 + y_lo), z: 4, core: 2. Of those that a mesh axis runs over, the one named last changes fastest.
Arguments:
- tokens: bfloat16 [8192, 2048], P(('ctx', 'tp')), may hold values from -6 to 6
- norm_gain: float32 [2048], replicated, may hold values from 0.5 to 1.5
- w_query: bfloat16 [2048, 2048], P('ctx', 'tp'), may hold values from -0.125 to 0.125
- key_matrix: bfloat16 [2048, 1024], P('ctx', 'tp'), may hold values from -0.125 to 0.125
- value_matrix: bfloat16 [2048, 1024], P('ctx', 'tp'), may hold values from -0.125 to 0.125
- query_gain: float32 [128], replicated, may hold values from 1 to 2
- key_gain: float32 [128], replicated, may hold values from 1 to 2
- w_out: bfloat16 [2048, 2048], P('ctx', 'tp'), may hold values from -0.5 to 0.5
- ffn_gain: float32 [2048], replicated, may hold values from 0.5 to 1.5
- w_gate: bfloat16 [2048, 6144], P('ctx', 'tp'), may hold values from -0.125 to 0.125
- w_up: bfloat16 [2048, 6144], P('ctx', 'tp'), may hold values from -0.125 to 0.125
- w_down: bfloat16 [2048, 6144], P('ctx', 'tp'), may hold values from -0.078125 to 0.078125
- cotangent: bfloat16 [8192, 2048], P(('ctx', 'tp')), may hold values from -6 to 6
Outputs:
- result: bfloat16 [8192, 2048], P(('ctx', 'tp'))
- grad_input: float32 [8192, 2048], P(('ctx', 'tp'))
- grad_norm_gain: float32 [2048], replicated
- grad_query: float32 [2048, 2048], P('ctx', 'tp')
- grad_key: float32 [2048, 1024], P('ctx', 'tp')
- grad_value: float32 [2048, 1024], P('ctx', 'tp')
- grad_query_gain: float32 [128], replicated
- grad_key_gain: float32 [128], replicated
- grad_out: float32 [2048, 2048], P('ctx', 'tp')
- grad_ffn_gain: float32 [2048], replicated
- grad_gate: float32 [2048, 6144], P('ctx', 'tp')
- grad_up: float32 [2048, 6144], P('ctx', 'tp')
- grad_down: float32 [2048, 6144], P('ctx', 'tp')
All inputs are finite; a program needn't handle non-finite values.
Results may differ from a plain program's by a relative error of at most 0.019.
Values may be sent and summed in bfloat16 or wider, within the bound.
A program may use at most 384 MiB of HBM per device.

v0:
```python
import math

import jax
import jax.numpy as jnp
from jax import lax
from jax.sharding import PartitionSpec as P

HEAD_DIMENSION = 128


epsilon = 1e-06
rope_base = 1000000.0
masked_score = -1e30


def rotate(value_rows, cosine, sine_table):
    middle = value_rows.shape[-1] // 2
    first_half = value_rows[..., :middle]
    second_half = value_rows[..., middle:]
    return jnp.concatenate(
        [
            first_half * cosine - second_half * sine_table,
            second_half * cosine + first_half * sine_table,
        ],
        axis=-1,
    )


def rope_tables(positions):
    exponent = jnp.arange(0, HEAD_DIMENSION, 2, dtype=jnp.float32) / HEAD_DIMENSION
    angles = positions[:, None] * (1.0 / rope_base**exponent)[None, :]
    return (jnp.cos(angles)[:, None, :], jnp.sin(angles)[:, None, :])


def norm_forward(value_rows):
    inverse = lax.rsqrt(jnp.mean(value_rows * value_rows, axis=-1, keepdims=True) + epsilon)
    return (value_rows * inverse, inverse)


def norm_backward(upstream, normal, inverse, gain):
    scaled = upstream * gain
    return inverse * (scaled - normal * jnp.mean(scaled * normal, axis=-1, keepdims=True))


def cross_rows(left_side, right_side):
    return lax.dot_general(
        left_side, right_side, (((1,), (1,)), ((), ())), preferred_element_type=jnp.float32
    )


def over_tokens(left_side, right_side):
    return lax.dot_general(
        left_side, right_side, (((0,), (0,)), ((), ())), preferred_element_type=jnp.float32
    )


def gather_rows(value_rows):
    return lax.all_gather(value_rows, "tp", axis=0, tiled=True)


def sum_rows(partial_sum):
    return lax.psum_scatter(
        partial_sum.astype(jnp.bfloat16), "tp", scatter_dimension=0, tiled=True
    ).astype(jnp.float32)


def fold_down(w_down, folder, initial):
    return folder(initial, lax.all_gather(w_down, "ctx", axis=0, tiled=True), jnp.int32(0))


def local(
    tokens,
    norm_gain,
    w_query,
    key_matrix,
    value_matrix,
    query_gain,
    key_gain,
    w_out,
    ffn_gain,
    w_gate,
    w_up,
    w_down,
    cotangent,
):
    tp_count = lax.axis_size("tp")
    ctx_count = lax.axis_size("ctx")
    block_tokens = tokens.shape[0] * tp_count
    seq_tokens = block_tokens * ctx_count
    query_cols = w_query.shape[1]
    kv_cols = key_matrix.shape[1]
    ffn_cols = w_gate.shape[1]
    kv_heads = kv_cols // HEAD_DIMENSION
    heads_per_group = query_cols // kv_cols
    local_heads = query_cols // HEAD_DIMENSION
    first_token = lax.axis_index("ctx") * block_tokens
    score_scale = HEAD_DIMENSION ** (-0.5)
    block_keys = math.gcd(seq_tokens, 512)
    state = tokens.astype(jnp.float32)
    normal_one, inverse_one = norm_forward(state)
    normalized_input = (normal_one * norm_gain).astype(jnp.bfloat16)
    normed_all = gather_rows(normalized_input)
    qkv_local = jnp.concatenate([w_query, key_matrix, value_matrix], axis=1)
    columns = normed_all
    projected = jnp.dot(
        columns,
        lax.all_gather(qkv_local, "ctx", axis=0, tiled=True),
        preferred_element_type=jnp.float32,
    )
    query_pre = projected[:, :query_cols].reshape(block_tokens, local_heads, HEAD_DIMENSION)
    key_pre = projected[:, query_cols : query_cols + kv_cols].reshape(
        block_tokens, kv_heads, HEAD_DIMENSION
    )
    value_bf = projected[:, query_cols + kv_cols :].astype(jnp.bfloat16)
    row_places = first_token + jnp.arange(block_tokens)
    cosine, sine_table = rope_tables(row_places.astype(jnp.float32))
    query_normal, query_inverse = norm_forward(query_pre)
    key_normal, key_inverse = norm_forward(key_pre)
    query_rot = rotate(query_normal * query_gain, cosine, sine_table).astype(jnp.bfloat16)
    key_rot = rotate(key_normal * key_gain, cosine, sine_table).astype(jnp.bfloat16)
    packed = jnp.concatenate([key_rot.reshape(block_tokens, kv_cols), value_bf], axis=1)
    packed_all = lax.all_gather(packed, "ctx", axis=0, tiled=True)
    grouped_heads = query_rot.reshape(block_tokens, kv_heads, heads_per_group, HEAD_DIMENSION)
    needed = (first_token + block_tokens + block_keys - 1) // block_keys

    def block_scores(index):
        start_key = index * block_keys
        key_block = lax.dynamic_slice_in_dim(packed_all, start_key, block_keys, 0)
        key_part = key_block[:, :kv_cols].reshape(block_keys, kv_heads, HEAD_DIMENSION)
        value_part = key_block[:, kv_cols:].reshape(block_keys, kv_heads, HEAD_DIMENSION)
        scores = (
            jnp.einsum(
                "qgnd,kgd->gnqk", grouped_heads, key_part, preferred_element_type=jnp.float32
            )
            * score_scale
        )
        allowed = row_places[:, None] >= (start_key + jnp.arange(block_keys))[None, :]
        return (jnp.where(allowed, scores, masked_score), key_part, value_part)

    def stats_step(index, carry):
        score_max, score_sum = carry
        scores, key_part, value_part = block_scores(index)
        new_max = jnp.maximum(score_max, jnp.max(scores, axis=-1))
        score_sum = score_sum * jnp.exp(score_max - new_max) + jnp.sum(
            jnp.exp(scores - new_max[..., None]), axis=-1
        )
        return (new_max, score_sum)

    stats_shape = (kv_heads, heads_per_group, block_tokens)
    score_max, score_sum = lax.fori_loop(
        0,
        needed,
        stats_step,
        (jnp.full(stats_shape, masked_score, jnp.float32), jnp.zeros(stats_shape, jnp.float32)),
    )
    log_total = score_max + jnp.log(score_sum)

    def value_step(index, accum):
        scores, key_part, value_part = block_scores(index)
        weights_bf = jnp.exp(scores - log_total[..., None]).astype(jnp.bfloat16)
        return accum + jnp.einsum(
            "gnqk,kgd->gnqd", weights_bf, value_part, preferred_element_type=jnp.float32
        )

    attended = lax.fori_loop(
        0,
        needed,
        value_step,
        jnp.zeros((kv_heads, heads_per_group, block_tokens, HEAD_DIMENSION), jnp.float32),
    )
    attended = attended.transpose(2, 0, 1, 3).reshape(block_tokens, query_cols)
    context_bf = attended.astype(jnp.bfloat16)
    attn_part = cross_rows(context_bf, lax.all_gather(w_out, "ctx", axis=0, tiled=True))
    middle_state = state + sum_rows(attn_part)
    normal_two, inverse_two = norm_forward(middle_state)
    normed_two = (normal_two * ffn_gain).astype(jnp.bfloat16)
    normed_two_all = gather_rows(normed_two)
    gate_up_local = jnp.concatenate([w_gate, w_up], axis=1)
    columns = normed_two_all
    gate_up = jnp.dot(
        columns,
        lax.all_gather(gate_up_local, "ctx", axis=0, tiled=True),
        preferred_element_type=jnp.float32,
    )
    gate_value = gate_up[:, :ffn_cols]
    upward = gate_up[:, ffn_cols:]
    sigmoid_gate = jax.nn.sigmoid(gate_value)
    activated = gate_value * sigmoid_gate
    hidden = (activated * upward).astype(jnp.bfloat16)
    grad_all = gather_rows(cotangent)
    ffn_part = cross_rows(hidden, lax.all_gather(w_down, "ctx", axis=0, tiled=True))

    def add_down(running, weight_piece, start_row):
        return jnp.dot(grad_all, weight_piece, preferred_element_type=jnp.float32)

    grad_hidden = fold_down(w_down, add_down, jnp.zeros((block_tokens, ffn_cols), jnp.float32))
    result = (middle_state + sum_rows(ffn_part)).astype(jnp.bfloat16)
    grad_gate = grad_hidden * upward * (sigmoid_gate * (1.0 + gate_value * (1.0 - sigmoid_gate)))
    grad_upward = grad_hidden * activated
    grad_gate_up = jnp.concatenate([grad_gate, grad_upward], axis=1).astype(jnp.bfloat16)
    back_two = cross_rows(grad_gate_up, lax.all_gather(gate_up_local, "ctx", axis=0, tiled=True))
    grad_normed_two = sum_rows(back_two)
    grad_middle = cotangent.astype(jnp.float32) + norm_backward(
        grad_normed_two, normal_two, inverse_two, ffn_gain
    )
    gain_two = jnp.sum(grad_normed_two * normal_two, axis=0)
    grad_middle_all = gather_rows(grad_middle.astype(jnp.bfloat16))
    columns = grad_middle_all
    grad_context = jnp.dot(
        columns,
        lax.all_gather(w_out, "ctx", axis=0, tiled=True),
        preferred_element_type=jnp.float32,
    )
    grad_context_bf = grad_context.astype(jnp.bfloat16)
    grad_grouped = grad_context_bf.reshape(block_tokens, kv_heads, heads_per_group, HEAD_DIMENSION)
    attended_grouped = attended.reshape(block_tokens, kv_heads, heads_per_group, HEAD_DIMENSION)
    row_delta = jnp.einsum("qgnd,qgnd->gnq", grad_grouped.astype(jnp.float32), attended_grouped)

    def score_grads(index):
        scores, key_part, value_part = block_scores(index)
        weights_full = jnp.exp(scores - log_total[..., None])
        grad_weights = jnp.einsum(
            "qgnd,kgd->gnqk", grad_grouped, value_part, preferred_element_type=jnp.float32
        )
        grad_scores = (weights_full * (grad_weights - row_delta[..., None])).astype(jnp.bfloat16)
        return (weights_full, grad_scores, key_part)

    query_zero = jnp.zeros((kv_heads, heads_per_group, block_tokens, HEAD_DIMENSION), jnp.float32)

    def grad_step(index, carry):
        grad_query_acc, grad_packed = carry
        weights_full, grad_scores, key_part = score_grads(index)
        grad_query_acc = (
            grad_query_acc
            + jnp.einsum(
                "gnqk,kgd->gnqd", grad_scores, key_part, preferred_element_type=jnp.float32
            )
            * score_scale
        )
        grad_key_block = (
            jnp.einsum(
                "gnqk,qgnd->kgd", grad_scores, grouped_heads, preferred_element_type=jnp.float32
            )
            * score_scale
        )
        grad_value_block = jnp.einsum(
            "gnqk,qgnd->kgd",
            weights_full.astype(jnp.bfloat16),
            grad_grouped,
            preferred_element_type=jnp.float32,
        )
        update = jnp.concatenate(
            [
                grad_key_block.reshape(block_keys, kv_cols),
                grad_value_block.reshape(block_keys, kv_cols),
            ],
            axis=1,
        )
        grad_packed = lax.dynamic_update_slice_in_dim(grad_packed, update, index * block_keys, 0)
        return (grad_query_acc, grad_packed)

    grad_query_acc, grad_packed = lax.fori_loop(
        0, needed, grad_step, (query_zero, jnp.zeros((seq_tokens, 2 * kv_cols), jnp.float32))
    )
    grad_own = lax.psum_scatter(grad_packed, "ctx", scatter_dimension=0, tiled=True)
    grad_key_rot = grad_own[:, :kv_cols].reshape(block_tokens, kv_heads, HEAD_DIMENSION)
    grad_value_bf = grad_own[:, kv_cols:].astype(jnp.bfloat16)
    grad_query_rot = grad_query_acc.transpose(2, 0, 1, 3).reshape(
        block_tokens, local_heads, HEAD_DIMENSION
    )
    grad_query_norm = rotate(grad_query_rot, cosine, -sine_table)
    grad_key_norm = rotate(grad_key_rot, cosine, -sine_table)
    gain_query = jnp.sum(grad_query_norm * query_normal, axis=(0, 1))
    gain_key = jnp.sum(grad_key_norm * key_normal, axis=(0, 1))
    grad_query_pre = norm_backward(
        grad_query_norm, query_normal, query_inverse, query_gain
    ).reshape(block_tokens, query_cols)
    grad_key_pre = norm_backward(grad_key_norm, key_normal, key_inverse, key_gain).reshape(
        block_tokens, kv_cols
    )
    grad_projected = jnp.concatenate(
        [grad_query_pre.astype(jnp.bfloat16), grad_key_pre.astype(jnp.bfloat16), grad_value_bf],
        axis=1,
    )
    back_one = cross_rows(grad_projected, lax.all_gather(qkv_local, "ctx", axis=0, tiled=True))
    grad_normed = sum_rows(back_one)
    grad_input = grad_middle + norm_backward(grad_normed, normal_one, inverse_one, norm_gain)
    gain_one = jnp.sum(grad_normed * normal_one, axis=0)
    pieces = [
        over_tokens(normed_all, grad_projected),
        over_tokens(grad_middle_all, context_bf),
        over_tokens(normed_two_all, grad_gate_up),
        over_tokens(grad_all, hidden),
    ]
    weight_grads = lax.psum_scatter(
        jnp.concatenate(pieces, axis=1), "ctx", scatter_dimension=0, tiled=True
    )
    offset_value = query_cols + kv_cols
    offset_out = offset_value + kv_cols
    offset_gate = offset_out + query_cols
    offset_up = offset_gate + ffn_cols
    offset_down = offset_up + ffn_cols
    gain_one, gain_two, gain_query, gain_key = lax.psum(
        (gain_one, gain_two, gain_query, gain_key), ("ctx", "tp")
    )
    return (
        result,
        grad_input,
        gain_one,
        weight_grads[:, :query_cols],
        weight_grads[:, query_cols:offset_value],
        weight_grads[:, offset_value:offset_out],
        gain_query,
        gain_key,
        weight_grads[:, offset_out:offset_gate],
        gain_two,
        weight_grads[:, offset_gate:offset_up],
        weight_grads[:, offset_up:offset_down],
        weight_grads[:, offset_down:],
    )


def solution(mesh):
    placed = (
        P(("ctx", "tp"), None),
        P(),
        P("ctx", "tp"),
        P("ctx", "tp"),
        P("ctx", "tp"),
        P(),
        P(),
        P("ctx", "tp"),
        P(),
        P("ctx", "tp"),
        P("ctx", "tp"),
        P("ctx", "tp"),
        P(("ctx", "tp"), None),
    )
    return jax.shard_map(
        local,
        mesh=mesh,
        in_specs=placed,
        out_specs=(
            P(("ctx", "tp"), None),
            P(("ctx", "tp"), None),
            P(),
            P("ctx", "tp"),
            P("ctx", "tp"),
            P("ctx", "tp"),
            P(),
            P(),
            P("ctx", "tp"),
            P(),
            P("ctx", "tp"),
            P("ctx", "tp"),
            P("ctx", "tp"),
        ),
        check_vma=False,
    )
```

profile of v0, /device:TPU:17, one launch (start us, length us, event | category | flops | bytes accessed | tf_op | source)
XLA Modules:
  0.0 1917.3 jit_solution(6950586681050860119)
XLA Ops:
  11.1 9.4 all_gather.31
  21.4 102.4 %all-gather.6.cloned.1.call-done = bf16[2048,2048]{1,0:T(8,128)(2,1)} async-done(((bf16[32,2048]{1,0:T(8,128)(2,1)}), bf16[2048,2048]{1,0:T(8,128)(2,1)}) %all-gather.6.cloned.1.call-update) | async-done | bytes 8388624 | tf_op jit(solution)/shard_map/all_gather | solution.py:107
  133.2 119.4 %all-gather.8.cloned.1.call-done = bf16[8192,1024]{1,0:T(8,128)(2,1)} async-done(((bf16[128,1024]{1,0:T(8,128)(2,1)}), bf16[8192,1024]{1,0:T(8,128)(2,1)}) %all-gather.8.cloned.1.call-update) | async-done | bytes 16777232 | tf_op jit(solution)/shard_map/all_gather | solution.py:122
  252.6 20.8 %copy.109 = bf16[8192,1024]{0,1:T(8,128)(2,1)} copy(bf16[8192,1024]{1,0:T(8,128)(2,1)} %all-gather.8.cloned.1.call-done) | data formatting | bytes 33554432
  278.6 80.9 %all-gather.10.cloned.1.call-done = bf16[2048,1024]{1,0:T(8,128)(2,1)} async-done(((bf16[32,1024]{1,0:T(8,128)(2,1)}), bf16[2048,1024]{1,0:T(8,128)(2,1)}) %all-gather.10.cloned.1.call-update) | async-done | bytes 4194320 | tf_op jit(solution)/shard_map/all_gather | solution.py:173
  365.6 12.4 all_gather.38
  384.9 9.8 all_gather.35
  394.7 133.7 %all-gather.12.cloned.1.call-done = bf16[2048,6144]{1,0:T(8,128)(2,1)} async-done(((bf16[32,6144]{1,0:T(8,128)(2,1)}), bf16[2048,6144]{1,0:T(8,128)(2,1)}) %all-gather.12.cloned.1.call-update) | async-done | bytes 25165840 | tf_op jit(solution)/shard_map/all_gather | solution.py:182
  528.4 13.2 fusion.67
  541.7 107.0 %all-gather.14.cloned.1.call-done = bf16[2048,3072]{1,0:T(8,128)(2,1)} async-done(((bf16[32,3072]{1,0:T(8,128)(2,1)}), bf16[2048,3072]{1,0:T(8,128)(2,1)}) %all-gather.14.cloned.1.call-update) | async-done | bytes 12582928 | tf_op jit(solution)/shard_map/all_gather | solution.py:191
  648.6 9.3 multiply_convert_fusion.1
  657.9 14.3 convolution_convert_fusion.3
  672.3 14.8 reduce-scatter.11.cloned.1.call-done
  690.1 9.5 all_gather.39
  704.4 11.3 broadcast_in_dim.34.clone
  715.7 9.4 while.39
  726.6 19.4 %fusion.27 = f32[2048,6144]{1,0:T(8,128)} fusion(bf16[128,2048]{1,0:T(8,128)(2,1)S(1)} %copy-done.13, bf16[128,3072]{1,0:T(8,128)(2,1)S(1)} %copy-done.26, bf16[128,3072]{1,0:T(8,128)(2,1)S(1)} %copy-done.25), kind=kOutput, calls=%fused_computation.58 | convolution fusion | flops 3224371200 | bytes 52428800 | tf_op jit(solution)/shard_map/dot_general | solution.py:52
  749.1 451.9 %reduce-scatter.13.cloned.1.call-done = f32[128,1024]{1,0:T(8,128)} async-done(((f32[8192,1024]{1,0:T(8,128)}), f32[128,1024]{1,0:T(8,128)}) %reduce-scatter.13.cloned.1.call-update) | async-done | bytes 524304 | tf_op jit(solution)/shard_map/reduce_scatter | solution.py:265
  1204.4 7.2 convolution_convert_fusion
  1211.9 10.2 convolution_bitcast_fusion.1
  1222.1 9.8 convolution_convert_fusion.1
  1236.4 8.1 fusion.54
  1244.6 66.4 %pad_maximum_fusion.1 = f32[2048,12288]{1,0:T(8,128)} fusion(f32[2048,3072]{1,0:T(8,128)} %convolution_bitcast_fusion.1, f32[2048,6144]{1,0:T(8,128)} %fusion.27, f32[2048,1024]{1,0:T(8,128)} %fusion.68, f32[2048,2048]{1,0:T(8,128)} %fusion.54), kind=kLoop, calls=%fused_computation.45 | loop fusion | flops 75497472 | bytes 201326592 | tf_op jit(solution)/shard_map/concatenate | solution.py:296
  1313.2 589.3 %all-reduce = (f32[2048]{0:T(1024)}, f32[128]{0:T(128)}, f32[128]{0:T(128)}, f32[2048]{0:T(1024)}) all-reduce(f32[2048]{0:T(1024)S(1)} %get-tuple-element.307, f32[128]{0:T(128)S(1)} %bitcast_reduce_fusion, f32[128]{0:T(128)S(1)} %bitcast_reduce_fusion.1, f32[2048]{0:T(1024)S(1)} %copy-done.34), channel_id=1, replica_groups=mesh['ctx'=64,'tp'=2] {'ctx','tp'}, use_global_device_ids=true, to_apply=%region_22.23 | all-reduce | flops 4352 | bytes 34816 | tf_op jit(solution)/shard_map/psum | solution.py:303
  (222 shorter events, 76.5 us)
Async XLA Ops:
  7.2 116.6 %all-gather.6.cloned.1.call-start = ((), (), s32[]{:S(2)}) async-start(), calls=%async_computation.6 | async-start | bytes 8519680 | tf_op jit(solution)/shard_map/all_gather | solution.py:107
  8.8 243.8 %all-gather.8.cloned.1.call-start = ((), (), s32[]{:S(2)}) async-start(), calls=%async_computation.7 | async-start | bytes 17039360 | tf_op jit(solution)/shard_map/all_gather | solution.py:122
  20.5 108.0 %copy-start.6 = (bf16[128,2048]{1,0:T(8,128)(2,1)}, bf16[128,2048]{1,0:T(8,128)(2,1)S(1)}, u32[]{:S(2)}) copy-start(bf16[128,2048]{1,0:T(8,128)(2,1)S(1)} %all_gather.31) | copy-start | bytes 1572868
  21.4 107.4 %copy-start.38 = (f32[128]{0:T(128)S(1)}, f32[128]{0:T(128)}, u32[]{:S(2)}) copy-start(f32[128]{0:T(128)} %param.25) | copy-start | bytes 1540
  130.3 229.1 %all-gather.10.cloned.1.call-start = ((), (), s32[]{:S(2)}) async-start(), calls=%async_computation.8 | async-start | bytes 4259840 | tf_op jit(solution)/shard_map/all_gather | solution.py:173
  131.1 251.6 %reduce-scatter.7.cloned.1.call-start = ((), (), s32[]{:S(2)}) async-start(), calls=%async_computation.9 | async-start | bytes 786432 | tf_op jit(solution)/shard_map/reduce_scatter | solution.py:62
  364.1 164.3 %all-gather.12.cloned.1.call-start = ((), (), s32[]{:S(2)}) async-start(), calls=%async_computation.10 | async-start | bytes 25559040 | tf_op jit(solution)/shard_map/all_gather | solution.py:182
  365.0 283.7 %all-gather.14.cloned.1.call-start = ((), (), s32[]{:S(2)}) async-start(), calls=%async_computation.11 | async-start | bytes 12779520 | tf_op jit(solution)/shard_map/all_gather | solution.py:191
  365.6 321.6 %reduce-scatter.11.cloned.1.call-start = ((), (), s32[]{:S(2)}) async-start(), calls=%async_computation.13 | async-start | bytes 786432 | tf_op jit(solution)/shard_map/reduce_scatter | solution.py:62
  378.0 270.6 %copy-start.20 = (bf16[128,2048]{1,0:T(8,128)(2,1)}, bf16[128,2048]{1,0:T(8,128)(2,1)S(1)}, u32[]{:S(2)}) copy-start(bf16[128,2048]{1,0:T(8,128)(2,1)S(1)} %all_gather.38) | copy-start | bytes 1572868
  383.8 305.1 %copy-start.35 = (f32[64]{0:T(128)}, f32[64]{0:T(128)S(1)}, u32[]{:S(2)}) copy-start(f32[64]{0:T(128)S(1)} %add_rsqrt_fusion.2) | copy-start | bytes 772
  394.7 147.0 %copy-start.12 = (bf16[128,2048]{1,0:T(8,128)(2,1)}, bf16[128,2048]{1,0:T(8,128)(2,1)S(1)}, u32[]{:S(2)}) copy-start(bf16[128,2048]{1,0:T(8,128)(2,1)S(1)} %all_gather.35) | copy-start | bytes 1572868
  672.2 528.7 %reduce-scatter.13.cloned.1.call-start = ((), (), s32[]{:S(2)}) async-start(), calls=%async_computation.14 | async-start | bytes 34078720 | tf_op jit(solution)/shard_map/reduce_scatter | solution.py:265
  725.1 586.1 %reduce-scatter.15.cloned.1.call-start = ((), (), s32[]{:S(2)}) async-start(), calls=%async_computation.15 | async-start | bytes 786432 | tf_op jit(solution)/shard_map/reduce_scatter | solution.py:62
  748.2 453.8 %copy-start.28 = (f32[128,64]{1,0:T(8,128)S(1)}, f32[128,64]{1,0:T(8,128)}, u32[]{:S(2)}) copy-start(f32[128,64]{1,0:T(8,128)} %get-tuple-element.397) | copy-start | bytes 98308
  748.6 453.7 %copy-start.23 = (f32[128,4]{1,0:T(8,128)S(1)}, f32[128,4]{1,0:T(8,128)}, u32[]{:S(2)}) copy-start(f32[128,4]{1,0:T(8,128)} %copy-done.22) | copy-start | bytes 6148
  1211.5 691.0 %reduce-scatter.9.cloned.1.call-start = ((), (), s32[]{:S(2)}) async-start(), calls=%async_computation.12 | async-start | bytes 786432 | tf_op jit(solution)/shard_map/reduce_scatter | solution.py:62
  1231.9 673.0 %reduce-scatter.17.cloned.1.call-start = ((), (), s32[]{:S(2)}) async-start(), calls=%async_computation.16 | async-start | bytes 102236160 | tf_op jit(solution)/shard_map/reduce_scatter | solution.py:295
  1311.0 591.5 %copy-start.9 = (bf16[64,2048]{1,0:T(8,128)(2,1)S(1)}, bf16[64,2048]{1,0:T(8,128)(2,1)}, u32[]{:S(2)}) copy-start(bf16[64,2048]{1,0:T(8,128)(2,1)} %reduce-scatter.7.cloned.1.call-done) | copy-start | bytes 786436
  1311.0 591.5 %copy-start.16 = (bf16[64,2048]{1,0:T(8,128)(2,1)S(1)}, bf16[64,2048]{1,0:T(8,128)(2,1)}, u32[]{:S(2)}) copy-start(bf16[64,2048]{1,0:T(8,128)(2,1)} %param.31) | copy-start | bytes 786436
  1311.0 591.5 %copy-start.17 = (bf16[64,2048]{1,0:T(8,128)(2,1)S(1)}, bf16[64,2048]{1,0:T(8,128)(2,1)}, u32[]{:S(2)}) copy-start(bf16[64,2048]{1,0:T(8,128)(2,1)} %reduce-scatter.11.cloned.1.call-done) | copy-start | bytes 786436
  1311.0 591.5 %copy-start.32 = (f32[2048]{0:T(1024)S(1)}, f32[2048]{0:T(1024)}, u32[]{:S(2)}) copy-start(f32[2048]{0:T(1024)} %param.27) | copy-start | bytes 24580
  1311.0 591.5 %copy-start.36 = (f32[64]{0:T(128)S(1)}, f32[64]{0:T(128)}, u32[]{:S(2)}) copy-start(f32[64]{0:T(128)} %copy-done.35) | copy-start | bytes 772
  1311.0 591.5 %copy-start.45 = (f32[64]{0:T(128)S(1)}, f32[64]{0:T(128)}, u32[]{:S(2)}) copy-start(f32[64]{0:T(128)} %copy-done.44) | copy-start | bytes 772
  (33 other events, 357.3 us)
Sparse Core Ops, SparseCore 0:
  10.3 113.4 all-gather.5
  130.5 122.0 all-gather.7
  254.3 105.1 all-gather.9
  364.2 18.3 reduce-scatter.6
  384.9 143.4 all-gather.11
  530.1 118.4 all-gather.13
  672.4 14.7 reduce-scatter.10
  725.2 475.6 reduce-scatter.12
  1211.7 17.0 reduce-scatter.14
  1232.0 17.1 reduce-scatter.8
  1311.2 545.6 reduce-scatter.16
where the time goes:
time: 1930 us; the launch traced here: 1920 us
  waiting for transfers between devices  1020 us (53%)
  blocking collectives  630 us (33%)
  matrix products  112 us (6%)
  other arithmetic  88.1 us (5%)
  local copies, waits for them, and re-layouts  54.1 us (3%)
    psum x1, blocking collectives, local(): lax.psum((gain_one, gain_two, gain_query, gain_key), ('ctx', 'tp'))  589 us
    reduce_scatter x1, waiting for transfers between devices, local(): lax.psum_scatter(grad_packed, 'ctx', scatter_dimension=0, tiled=True)  452 us
    all_gather x1, waiting for transfers between devices, local(): lax.all_gather(gate_up_local, 'ctx', axis=0, tiled=True)  134 us
    all_gather x1, waiting for transfers between devices, local(): packed_all = lax.all_gather(packed, 'ctx', axis=0, tiled=True)  119 us
    all_gather x1, waiting for transfers between devices, local(): lax.all_gather(w_down, 'ctx', axis=0, tiled=True)  107 us
    all_gather x1, waiting for transfers between devices, local(): lax.all_gather(qkv_local, 'ctx', axis=0, tiled=True)  102 us
    all_gather x1, waiting for transfers between devices, local(): lax.all_gather(w_out, 'ctx', axis=0, tiled=True)  80.9 us
    concatenate x1, other arithmetic, local(): jnp.concatenate(pieces, axis=1)  66.4 us
  transfers between devices with their start and end apart: 11, of which 8 were waited for; matrix products, arithmetic and copies ran while one was open for 9% of the time, Pallas kernels for 0%

commit v1 on v0

v1 whole, which is shorter than its diff:
```python
import functools

import jax
import jax.numpy as jnp
from jax import lax
from jax.experimental import pallas as pl
from jax.experimental.pallas import tpu as pltpu
from jax.sharding import Mesh
from jax.sharding import PartitionSpec as P

AXES = ("z", "yl", "x", "c", "t")
SIZES = {"z": 4, "yl": 2, "x": 4, "c": 2, "t": 2}
W_AXES = ("z", "yl")
T_AXES = ("x", "c", "t")
NW, NT = 8, 16
ROWS = 64
TOK = NW * ROWS
D = 2048
HD = 128
SEQ = 8192
QC, KC, FC = 256, 128, 768
QKV = QC + 2 * KC
COLS = QKV + QC + 3 * FC
VMEM_LIMIT = 60 << 20

epsilon = 1e-06
rope_base = 1000000.0
score_scale = HD ** (-0.5)
LOG2E = 1.4426950408889634

bf16 = jnp.bfloat16
f32 = jnp.float32
MESH = pl.DeviceIdType.MESH
VM = pl.BlockSpec(memory_space=pltpu.VMEM)
ANY = pl.BlockSpec(memory_space=pl.ANY)
DMA = pltpu.SemaphoreType.DMA


def params(cid=None):
    if cid is None:
        return pltpu.CompilerParams(vmem_limit_bytes=VMEM_LIMIT)
    return pltpu.CompilerParams(
        collective_id=cid, has_side_effects=True, vmem_limit_bytes=VMEM_LIMIT
    )


def place():
    return {a: lax.axis_index(a) for a in AXES}


def shifted(me, axis, by):
    return lax.rem(me[axis] + by, SIZES[axis])


def barrier(devices):
    sem = pltpu.get_barrier_semaphore()
    for d in devices:
        pl.semaphore_signal(sem, inc=1, device_id=d, device_id_type=MESH)
    pl.semaphore_wait(sem, len(devices))


def remote(src, dst, ssem, rsem, device):
    return pltpu.make_async_remote_copy(
        src_ref=src, dst_ref=dst, send_sem=ssem, recv_sem=rsem, device_id=device, device_id_type=MESH
    )


class Sends:
    def __init__(self, ssem, rsem, base=0):
        self.ssem, self.rsem, self.base, self.open = ssem, rsem, base, []

    def send(self, kind, src, dst, device):
        k = self.base + kind
        c = remote(src, dst, self.ssem.at[k], self.rsem.at[k], device)
        c.start()
        self.open.append(c)

    def recv(self, kind, dst, device):
        k = self.base + kind
        remote(dst, dst, self.ssem.at[k], self.rsem.at[k], device).wait_recv()

    def close(self):
        for c in self.open:
            c.wait_send()


def w_devices(me):
    return (
        {"z": shifted(me, "z", 1)},
        {"z": shifted(me, "z", 3)},
        {"yl": 1 - me["yl"]},
    )


class GatherW:
    KINDS = 14

    def __init__(self, me, dst, sends):
        self.me, self.dst, self.s = me, dst, sends
        z, y = me["z"], me["yl"]
        zp, zm, zo, yo = shifted(me, "z", 1), shifted(me, "z", 3), shifted(me, "z", 2), 1 - y
        self.own, self.own_o = 2 * z + y, 2 * z + yo
        self.gp, self.gpo = 2 * zp + y, 2 * zp + yo
        self.gm, self.gmo = 2 * zm + y, 2 * zm + yo
        self.go, self.goo = 2 * zo + y, 2 * zo + yo
        self.dp, self.dm, self.dy = w_devices(me)

    def part(self, g, lo, hi):
        return self.dst.at[g, lo:hi]

    def put(self, kind, g, lo, hi, device):
        self.s.send(kind, self.part(g, lo, hi), self.part(g, lo, hi), device)

    def got(self, kind, g, lo, hi, device):
        self.s.recv(kind, self.part(g, lo, hi), device)

    def start(self):
        self.put(0, self.own, 0, 64, self.dp)
        self.put(1, self.own, 0, 64, self.dm)
        self.put(2, self.own, 0, 64, self.dy)

    def middle(self):
        dp, dm, dy = self.dp, self.dm, self.dy
        self.got(2, self.own_o, 0, 64, dy)
        self.put(3, self.own_o, 0, 32, dp)
        self.put(4, self.own_o, 0, 32, dm)
        self.got(0, self.gm, 0, 64, dm)
        self.put(5, self.gm, 16, 48, dp)
        self.put(6, self.gm, 32, 64, dy)
        self.got(1, self.gp, 0, 64, dp)
        self.put(7, self.gp, 0, 16, dm)
        self.put(8, self.gp, 48, 64, dm)
        self.put(9, self.gp, 32, 64, dy)

    def end(self):
        dp, dm, dy = self.dp, self.dm, self.dy
        self.got(3, self.gmo, 0, 32, dm)
        self.put(10, self.gmo, 16, 32, dp)
        self.got(4, self.gpo, 0, 32, dp)
        self.put(11, self.gpo, 0, 16, dm)
        self.got(5, self.go, 16, 48, dm)
        self.put(12, self.go, 32, 48, dy)
        self.got(8, self.go, 48, 64, dp)
        self.put(13, self.go, 48, 64, dy)
        self.got(7, self.go, 0, 16, dp)
        self.got(6, self.gmo, 32, 64, dy)
        self.got(9, self.gpo, 32, 64, dy)
        self.got(10, self.goo, 16, 32, dm)
        self.got(11, self.goo, 0, 16, dp)
        self.got(12, self.goo, 32, 48, dy)
        self.got(13, self.goo, 48, 64, dy)


class SumW:
    KINDS = 11
    LAND = (32, 32, 32, 16, 16, 32, 32, 32, 32, 64, 64, 64)

    def __init__(self, me, part, land, sends):
        self.part, self.land, self.s = part, land, sends
        z, y = me["z"], me["yl"]
        zp, zm, zo, yo = shifted(me, "z", 1), shifted(me, "z", 3), shifted(me, "z", 2), 1 - y
        self.own, self.own_o = 2 * z + y, 2 * z + yo
        self.gp, self.gpo = 2 * zp + y, 2 * zp + yo
        self.gm, self.gmo = 2 * zm + y, 2 * zm + yo
        self.go, self.goo = 2 * zo + y, 2 * zo + yo
        self.dp, self.dm, self.dy = w_devices(me)
        self.offset = [sum(self.LAND[:k]) for k in range(len(self.LAND))]

    def slot(self, kind, lo=0, n=None):
        n = self.LAND[kind] if n is None else n
        return self.land.at[self.offset[kind] + lo : self.offset[kind] + lo + n]

    def put(self, kind, g, lo, hi, device):
        self.s.send(kind, self.part.at[g, lo:hi], self.slot(kind), device)

    def got(self, kind, device):
        self.s.recv(kind, self.slot(kind), device)

    def add(self, kind, g, lo, hi):
        rows = self.slot(kind)
        self.part[g, lo:hi] = (self.part[g, lo:hi].astype(f32) + rows[...].astype(f32)).astype(bf16)

    def run(self):
        dp, dm, dy = self.dp, self.dm, self.dy
        self.put(0, self.goo, 32, 64, dy)
        self.put(3, self.goo, 16, 32, dm)
        self.put(4, self.goo, 0, 16, dp)
        self.put(1, self.gmo, 32, 64, dy)
        self.put(2, self.gpo, 32, 64, dy)
        self.got(0, dy)
        self.add(0, self.go, 32, 64)
        self.put(5, self.go, 16, 48, dm)
        self.s.send(6, self.part.at[self.go, 0:16], self.slot(6, 0, 16), dp)
        self.s.send(11, self.part.at[self.go, 48:64], self.slot(6, 16, 16), dp)
        self.got(3, dp)
        self.add(3, self.gmo, 16, 32)
        self.put(7, self.gmo, 0, 32, dm)
        self.got(4, dm)
        self.add(4, self.gpo, 0, 16)
        self.put(8, self.gpo, 0, 32, dp)
        self.got(1, dy)
        self.add(1, self.gm, 32, 64)
        self.got(5, dp)
        self.add(5, self.gm, 16, 48)
        self.put(9, self.gm, 0, 64, dm)
        self.got(2, dy)
        self.add(2, self.gp, 32, 64)
        self.s.recv(6, self.slot(6, 0, 16), dm)
        self.s.recv(11, self.slot(6, 16, 16), dm)
        lo, hi = self.slot(6, 0, 16), self.slot(6, 16, 16)
        self.part[self.gp, 0:16] = (self.part[self.gp, 0:16].astype(f32) + lo[...].astype(f32)).astype(bf16)
        self.part[self.gp, 48:64] = (self.part[self.gp, 48:64].astype(f32) + hi[...].astype(f32)).astype(bf16)
        self.put(10, self.gp, 0, 64, dp)
        self.got(7, dp)
        self.add(7, self.own_o, 0, 32)
        self.got(8, dm)
        self.add(8, self.own_o, 0, 32)
        self.s.send(12, self.part.at[self.own_o], self.slot(11), dy)
        self.got(9, dp)
        self.got(10, dm)
        self.s.recv(12, self.slot(11), dy)
        total = self.part[self.own].astype(f32) + self.slot(9)[...].astype(f32)
        return total + self.slot(10)[...].astype(f32) + self.slot(11)[...].astype(f32)


SUMW_ROWS = sum(SumW.LAND)
SUMW_SEMS = 13


def t_devices(me):
    return (
        {"x": shifted(me, "x", 1)},
        {"x": shifted(me, "x", 3)},
        {"t": 1 - me["t"]},
        {"c": 1 - me["c"]},
    )


class GatherT:
    KINDS = 19

    def __init__(self, me, dst, sends):
        self.dst, self.s = dst, sends
        x, c, t = me["x"], me["c"], me["t"]
        xp, xm, xo = shifted(me, "x", 1), shifted(me, "x", 3), shifted(me, "x", 2)

        def at(x, t, c=c):
            return (x * 2 + c) * 2 + t

        to = 1 - t
        self.ids = {
            "own": at(x, t), "to": at(x, to), "p": at(xp, t), "po": at(xp, to),
            "m": at(xm, t), "mo": at(xm, to), "o": at(xo, t), "oo": at(xo, to),
        }
        self.sib = {k: v + 2 * (1 - 2 * c) for k, v in self.ids.items()}
        self.dp, self.dm, self.dt, self.dc = t_devices(me)

    def part(self, s, half):
        lo, hi = {None: (0, 8), 0: (0, 4), 1: (4, 8)}[half]
        return self.dst.at[lo:hi, s]

    def put(self, kind, name, device, half=None):
        s = self.ids[name]
        self.s.send(kind, self.part(s, half), self.part(s, half), device)

    def got(self, kind, name, device, half=None, sib=False):
        s = (self.sib if sib else self.ids)[name]
        self.s.recv(kind, self.part(s, half), device)

    def start(self):
        self.put(2, "own", self.dt)
        self.put(0, "own", self.dp)
        self.put(1, "own", self.dm)
        self.put(3, "own", self.dc)

    def middle(self):
        dp, dm, dt, dc = self.dp, self.dm, self.dt, self.dc
        self.got(0, "m", dm)
        self.put(7, "m", dp, 0)
        self.put(8, "m", dc)
        self.got(1, "p", dp)
        self.put(9, "p", dm, 1)
        self.put(10, "p", dc)
        self.got(2, "to", dt)
        self.put(4, "to", dp)
        self.put(5, "to", dm)
        self.put(6, "to", dc)

    def end(self):
        dp, dm, dt, dc = self.dp, self.dm, self.dt, self.dc
        self.got(7, "o", dm, 0)
        self.put(15, "o", dc, 0)
        self.got(9, "o", dp, 1)
        self.put(16, "o", dc, 1)
        self.got(4, "mo", dm)
        self.put(11, "mo", dp, 0)
        self.put(12, "mo", dc)
        self.got(5, "po", dp)
        self.put(13, "po", dm, 1)
        self.put(14, "po", dc)
        self.got(11, "oo", dm, 0)
        self.put(17, "oo", dc, 0)
        self.got(13, "oo", dp, 1)
        self.put(18, "oo", dc, 1)
        for kind, name, half in (
            (3, "own", None), (8, "m", None), (10, "p", None), (6, "to", None), (15, "o", 0), (16, "o", 1),
            (12, "mo", None), (14, "po", None), (17, "oo", 0), (18, "oo", 1),
        ):
            self.got(kind, name, dc, half, True)


def sems(n):
    return [DMA((n,)), DMA((n,))]


def spread_kernel(normed_ref, stage_ref, normed_all, weights, rest, ssem, rsem, local):
    me = place()
    z, y, t = me["z"], me["yl"], me["t"]
    own_g = 2 * z + y
    s = (me["x"] * 2 + me["c"]) * 2 + t
    dp, dm, dy = w_devices(me)
    sem = pltpu.get_barrier_semaphore()
    for dz in range(4):
        for dyl in range(2):
            for dt in range(2):
                if dz or dyl or dt:
                    pl.semaphore_signal(
                        sem, inc=1, device_id_type=MESH,
                        device_id={
                            "z": shifted(me, "z", dz), "yl": shifted(me, "yl", dyl), "t": shifted(me, "t", dt)
                        },
                    )
    for d in t_devices(me)[:2] + t_devices(me)[3:]:
        pl.semaphore_signal(sem, inc=1, device_id=d, device_id_type=MESH)
    pl.semaphore_wait(sem, 18)

    mine = pltpu.make_async_copy(normed_ref, normed_all.at[own_g], local.at[0])
    mine.start()
    base_b = GatherW.KINDS
    base_c = base_b + 8
    for j in range(4):
        for t2 in range(2):
            g = 4 * t + j
            dst_z, dst_y = 2 * t + j // 2, j % 2
            is_me = (dst_z == z) & (dst_y == y) & (t == t2)
            src = stage_ref.at[j, 16 * t2 : 16 * t2 + 16]
            to = {"z": dst_z, "yl": dst_y, "t": jnp.int32(t2)}
            qk = remote(
                src.at[:, :QKV], weights.at[own_g, s - t + t2], ssem.at[base_b + j * 2 + t2],
                rsem.at[base_b + own_g], to,
            )
            ot = remote(
                src.at[:, QKV:], rest.at[own_g], ssem.at[base_c + j * 2 + t2], rsem.at[base_c + own_g], to,
            )
            lq = pltpu.make_async_copy(src.at[:, :QKV], weights.at[own_g, s], local.at[1])
            lo = pltpu.make_async_copy(src.at[:, QKV:], rest.at[own_g], local.at[2])

            @pl.when(is_me)
            def _():
                lq.start()
                lo.start()
                lq.wait()
                lo.wait()

            @pl.when(jnp.logical_not(is_me))
            def _():
                qk.start()
                ot.start()

    mine.wait()
    gw = GatherW(me, normed_all, Sends(ssem, rsem))
    gw.start()
    holder = own_g // 4
    for g in range(8):
        from_me = (own_g == g) & (holder == t)

        @pl.when(jnp.logical_not(from_me))
        def _(g=g):
            dst = weights.at[g, s]
            remote(dst, dst, ssem.at[0], rsem.at[base_b + g], dy).wait_recv()

    gt = GatherT(me, weights, Sends(ssem, rsem, base_c + 8))
    gt.start()
    gw.middle()
    gt.middle()
    gw.end()
    gt.end()
    for g in range(8):
        from_me = (own_g == g) & (holder == t)

        @pl.when(jnp.logical_not(from_me))
        def _(g=g):
            dst = rest.at[g]
            remote(dst, dst, ssem.at[0], rsem.at[base_c + g], dy).wait_recv()

    for j in range(4):
        for t2 in range(2):
            is_me = (2 * t + j // 2 == z) & (j % 2 == y) & (t == t2)

            @pl.when(jnp.logical_not(is_me))
            def _(j=j, t2=t2):
                src = stage_ref.at[j, 16 * t2 : 16 * t2 + 16]
                k = j * 2 + t2
                remote(src.at[:, :QKV], src.at[:, :QKV], ssem.at[base_b + k], rsem.at[0], dy).wait_send()
                remote(src.at[:, QKV:], src.at[:, QKV:], ssem.at[base_c + k], rsem.at[0], dy).wait_send()

    gw.s.close()
    gt.s.close()


def spread(normed, stage):
    n = GatherW.KINDS + 16 + GatherT.KINDS
    return pl.pallas_call(
        spread_kernel,
        out_shape=(
            jax.ShapeDtypeStruct((NW, ROWS, D), bf16),
            jax.ShapeDtypeStruct((NW, NT, 16, QKV), bf16),
            jax.ShapeDtypeStruct((NW, 16, COLS - QKV), bf16),
        ),
        in_specs=[VM, VM],
        out_specs=(VM, VM, VM),
        scratch_shapes=sems(n) + [DMA((3,))],
        compiler_params=params(0),
        name="spread",
    )(normed, stage)


def gather_kernel(x_ref, out, ssem, rsem, local):
    me = place()
    barrier(w_devices(me))
    mine = pltpu.make_async_copy(x_ref, out.at[2 * me["z"] + me["yl"]], local)
    mine.start()
    mine.wait()
    g = GatherW(me, out, Sends(ssem, rsem))
    g.start()
    g.middle()
    g.end()
    g.s.close()


def gather_rows(x, cid):
    out = pl.pallas_call(
        gather_kernel,
        out_shape=jax.ShapeDtypeStruct((NW,) + x.shape, x.dtype),
        in_specs=[VM],
        out_specs=VM,
        scratch_shapes=sems(GatherW.KINDS) + [DMA(())],
        compiler_params=params(cid),
        name="gather_rows",
    )(x)
    return out.reshape(TOK, x.shape[1])


def keys_kernel(kv_ref, cot_ref, kv_all, cot_all, ssem, rsem, local):
    me = place()
    barrier(t_devices(me) + w_devices(me))
    s = (me["x"] * 2 + me["c"]) * 2 + me["t"]
    a = pltpu.make_async_copy(kv_ref, kv_all.at[:, s], local.at[0])
    b = pltpu.make_async_copy(cot_ref, cot_all.at[2 * me["z"] + me["yl"]], local.at[1])
    a.start()
    b.start()
    a.wait()
    b.wait()
    gt = GatherT(me, kv_all, Sends(ssem, rsem))
    gw = GatherW(me, cot_all, Sends(ssem, rsem, GatherT.KINDS))
    gt.start()
    gw.start()
    gt.middle()
    gw.middle()
    gt.end()
    gw.end()
    gt.s.close()
    gw.s.close()


def gather_keys(kv, cot, cid):
    n = GatherT.KINDS + GatherW.KINDS
    kv_all, cot_all = pl.pallas_call(
        keys_kernel,
        out_shape=(
            jax.ShapeDtypeStruct((NW, NT, ROWS, 2 * KC), bf16),
            jax.ShapeDtypeStruct((NW, ROWS, D), bf16),
        ),
        in_specs=[VM, VM],
        out_specs=(VM, VM),
        scratch_shapes=sems(n) + [DMA((2,))],
        compiler_params=params(cid),
        name="gather_keys",
    )(kv.reshape(NW, ROWS, 2 * KC), cot)
    return kv_all.reshape(SEQ, 2 * KC), cot_all.reshape(TOK, D)


def sum_kernel(x_ref, out, part, land, ssem, rsem, local):
    me = place()
    barrier(w_devices(me))
    c = pltpu.make_async_copy(x_ref, part, local)
    c.start()
    c.wait()
    s = SumW(me, part, land, Sends(ssem, rsem))
    out[...] = s.run()
    s.s.close()


def sum_rows(x, cid):
    return pl.pallas_call(
        sum_kernel,
        out_shape=jax.ShapeDtypeStruct((ROWS, D), f32),
        in_specs=[VM],
        out_specs=VM,
        scratch_shapes=[pltpu.VMEM((NW, ROWS, D), bf16), pltpu.VMEM((SUMW_ROWS, D), bf16)]
        + sems(SUMW_SEMS) + [DMA(())],
        compiler_params=params(cid),
        name="sum_rows",
    )(x.astype(bf16).reshape(NW, ROWS, D))


def sum_keys_kernel(x_ref, out, part, half, land, final, ssem, rsem, local):
    me = place()
    barrier(t_devices(me))
    x, c, t = me["x"], me["c"], me["t"]
    xp, xm, xo = shifted(me, "x", 1), shifted(me, "x", 3), shifted(me, "x", 2)
    dp, dm, dt, dc = t_devices(me)
    s = Sends(ssem, rsem)
    order = (xo, xm, xp, x)
    for i, xi in enumerate(order):
        s.send(i, x_ref.at[:, xi, 1 - c], part.at[i], dc)
    for i, xi in enumerate(order):
        s.recv(i, part.at[i], dc)
        part[i] = (part[i].astype(f32) + x_ref[:, xi, c].astype(f32)).astype(bf16)
        if i == 0:
            s.send(4, part.at[0, 0:4], half.at[0], dm)
            s.send(5, part.at[0, 4:8], half.at[1], dp)
        if i == 1:
            s.recv(4, half.at[0], dp)
            part[1, 0:4] = (part[1, 0:4].astype(f32) + half[0].astype(f32)).astype(bf16)
            s.send(6, part.at[1], land.at[0], dm)
        if i == 2:
            s.recv(5, half.at[1], dm)
            part[2, 4:8] = (part[2, 4:8].astype(f32) + half[1].astype(f32)).astype(bf16)
            s.send(7, part.at[2], land.at[1], dp)
    s.recv(6, land.at[0], dp)
    s.recv(7, land.at[1], dm)
    to = 1 - t
    part[3, :, to] = (
        part[3, :, to].astype(f32) + land[0, :, to].astype(f32) + land[1, :, to].astype(f32)
    ).astype(bf16)
    s.send(8, part.at[3, :, to], final, dt)
    own = part[3, :, t].astype(f32) + land[0, :, t].astype(f32) + land[1, :, t].astype(f32)
    s.recv(8, final, dt)
    out[...] = own + final[...].astype(f32)
    s.close()


def sum_keys(x, cid):
    out = pl.pallas_call(
        sum_keys_kernel,
        out_shape=jax.ShapeDtypeStruct((NW, ROWS, 2 * KC), f32),
        in_specs=[VM],
        out_specs=VM,
        scratch_shapes=[
            pltpu.VMEM((4, NW, 2, ROWS, 2 * KC), bf16),
            pltpu.VMEM((2, 4, 2, ROWS, 2 * KC), bf16),
            pltpu.VMEM((2, NW, 2, ROWS, 2 * KC), bf16),
            pltpu.VMEM((NW, ROWS, 2 * KC), bf16),
        ]
        + sems(9) + [DMA(())],
        compiler_params=params(cid),
        name="sum_keys",
    )(x.reshape(NW, 4, 2, 2, ROWS, 2 * KC))
    return out.reshape(TOK, 2 * KC)


def return_kernel(x_ref, out, ssem, rsem, local):
    me = place()
    z, y, t = me["z"], me["yl"], me["t"]
    own_g = 2 * z + y
    sem = pltpu.get_barrier_semaphore()
    for dz in range(4):
        for dyl in range(2):
            for dt in range(2):
                if dz or dyl or dt:
                    pl.semaphore_signal(
                        sem, inc=1, device_id_type=MESH,
                        device_id={
                            "z": shifted(me, "z", dz), "yl": shifted(me, "yl", dyl), "t": shifted(me, "t", dt)
                        },
                    )
    pl.semaphore_wait(sem, 15)
    holder = own_g // 4
    block = own_g - 4 * holder
    for g in range(8):
        is_me = (own_g == g) & (holder == t)
        dst = out.at[block, t]
        to = {"z": jnp.int32(g // 2), "yl": jnp.int32(g % 2), "t": holder}
        c = remote(x_ref.at[g], dst, ssem.at[g], rsem.at[block * 2 + t], to)
        l = pltpu.make_async_copy(x_ref.at[g], dst, local)

        @pl.when(is_me)
        def _():
            l.start()
            l.wait()

        @pl.when(jnp.logical_not(is_me))
        def _():
            c.start()

    dy = w_devices(me)[2]
    for j in range(4):
        for t2 in range(2):
            is_me = (2 * t + j // 2 == z) & (j % 2 == y) & (t == t2)

            @pl.when(jnp.logical_not(is_me))
            def _(j=j, t2=t2):
                d = out.at[j, t2]
                remote(d, d, ssem.at[0], rsem.at[j * 2 + t2], dy).wait_recv()

    for g in range(8):
        is_me = (own_g == g) & (holder == t)

        @pl.when(jnp.logical_not(is_me))
        def _(g=g):
            remote(x_ref.at[g], x_ref.at[g], ssem.at[g], rsem.at[0], dy).wait_send()


def return_weights(x, cid):
    cols = x.shape[-1]
    return pl.pallas_call(
        return_kernel,
        out_shape=jax.ShapeDtypeStruct((4, 2, 16, cols), x.dtype),
        in_specs=[VM],
        out_specs=VM,
        scratch_shapes=sems(8) + [DMA(())],
        compiler_params=params(cid),
        name="return_weights",
    )(x)


KB = 256
CH = 2 * ROWS
NROW = NW * CH


def attend_kernel(q_ref, kv_ref, o_ref, l_ref):
    s = (lax.axis_index("x") * 2 + lax.axis_index("c")) * 2 + lax.axis_index("t")
    o_ref[...] = jnp.zeros_like(o_ref)
    l_ref[...] = jnp.zeros_like(l_ref)
    factor = score_scale * LOG2E
    for g in range(NW):
        first = g * CH

        def block(b, carry, g=g, first=first):
            keys = pl.ds(pl.multiple_of(g * 1024 + b * KB, KB), KB)
            k = kv_ref[keys, :KC]
            v = kv_ref[keys, KC:]
            for r0 in range(first, NROW, 256):
                r1 = min(r0 + 256, NROW)
                sc = lax.dot_general(
                    q_ref[r0:r1], k, (((1,), (1,)), ((), ())), preferred_element_type=f32
                )
                p = jnp.exp2(sc * factor)
                if r0 == first:
                    row = lax.broadcasted_iota(jnp.int32, (r1 - r0, KB), 0)
                    col = lax.broadcasted_iota(jnp.int32, (r1 - r0, KB), 1)
                    seen = (row >= CH) | (s * ROWS + (row & (ROWS - 1)) >= b * KB + col)
                    p = jnp.where(seen, p, 0.0)
                l_ref[r0:r1] += p[:, :128] + p[:, 128:]
                o_ref[r0:r1] += jnp.dot(p.astype(bf16), v, preferred_element_type=f32)
            return carry

        lax.fori_loop(0, 1024 // KB, block, 0)


def attend(q, kv_all):
    return pl.pallas_call(
        attend_kernel,
        out_shape=(
            jax.ShapeDtypeStruct((NROW, HD), f32),
            jax.ShapeDtypeStruct((NROW, HD), f32),
        ),
        in_specs=[VM, VM],
        out_specs=(VM, VM),
        compiler_params=params(),
        name="attend",
    )(q, kv_all)


def attend_back_kernel(q_ref, do_ref, lse_ref, delta_ref, kv_ref, dq_ref, dkv_ref):
    s = (lax.axis_index("x") * 2 + lax.axis_index("c")) * 2 + lax.axis_index("t")
    dq_ref[...] = jnp.zeros_like(dq_ref)
    factor = score_scale * LOG2E
    for g in range(NW):
        first = g * CH

        def block(b, carry, g=g, first=first):
            keys = pl.ds(pl.multiple_of(g * 1024 + b * KB, KB), KB)
            k = kv_ref[keys, :KC]
            v = kv_ref[keys, KC:]
            dk = jnp.zeros((KB, HD), f32)
            dv = jnp.zeros((KB, HD), f32)
            for r0 in range(first, NROW, 256):
                r1 = min(r0 + 256, NROW)
                q = q_ref[r0:r1]
                do = do_ref[r0:r1]
                sc = lax.dot_general(k, q, (((1,), (1,)), ((), ())), preferred_element_type=f32)
                p = jnp.exp2(sc * factor - lse_ref[:, r0:r1])
                if r0 == first:
                    row = lax.broadcasted_iota(jnp.int32, (KB, r1 - r0), 1)
                    col = lax.broadcasted_iota(jnp.int32, (KB, r1 - r0), 0)
                    seen = (row >= CH) | (s * ROWS + (row & (ROWS - 1)) >= b * KB + col)
                    p = jnp.where(seen, p, 0.0)
                dp = lax.dot_general(v, do, (((1,), (1,)), ((), ())), preferred_element_type=f32)
                ds = (p * (dp - delta_ref[:, r0:r1])).astype(bf16)
                dv = dv + jnp.dot(p.astype(bf16), do, preferred_element_type=f32)
                dk = dk + jnp.dot(ds, q, preferred_element_type=f32)
                dq_ref[r0:r1] += lax.dot_general(
                    ds, k, (((0,), (0,)), ((), ())), preferred_element_type=f32
                )
            dkv_ref[keys, :KC] = (dk * score_scale).astype(bf16)
            dkv_ref[keys, KC:] = dv.astype(bf16)
            return carry

        lax.fori_loop(0, 1024 // KB, block, 0)


def attend_back(q, do, lse, delta, kv_all):
    return pl.pallas_call(
        attend_back_kernel,
        out_shape=(
            jax.ShapeDtypeStruct((NROW, HD), f32),
            jax.ShapeDtypeStruct((SEQ, 2 * KC), bf16),
        ),
        in_specs=[VM] * 5,
        out_specs=(VM, VM),
        compiler_params=params(),
        name="attend_back",
    )(q, do, lse, delta, kv_all)


def rotate(value_rows, cosine, sine_table):
    middle = value_rows.shape[-1] // 2
    first_half = value_rows[..., :middle]
    second_half = value_rows[..., middle:]
    return jnp.concatenate(
        [
            first_half * cosine - second_half * sine_table,
            second_half * cosine + first_half * sine_table,
        ],
        axis=-1,
    )


def norm_forward(value_rows):
    inverse = lax.rsqrt(jnp.mean(value_rows * value_rows, axis=-1, keepdims=True) + epsilon)
    return (value_rows * inverse, inverse)


def norm_backward(upstream, normal, inverse, gain):
    scaled = upstream * gain
    return inverse * (scaled - normal * jnp.mean(scaled * normal, axis=-1, keepdims=True))


def cross_rows(left_side, right_side):
    return lax.dot_general(
        left_side, right_side, (((1,), (1,)), ((), ())), preferred_element_type=f32
    )


def over_tokens(left_side, right_side):
    return lax.dot_general(
        left_side, right_side, (((0,), (0,)), ((), ())), preferred_element_type=f32
    ).astype(bf16)


def to_rows(v):
    return v.reshape(NW, ROWS, 2, HD).transpose(0, 2, 1, 3).reshape(NROW, HD)


def from_rows(v):
    return v.reshape(NW, 2, ROWS, HD).transpose(0, 2, 1, 3).reshape(TOK, 2 * HD)


def gather_weight(w):
    return lax.all_gather(w, T_AXES, axis=1, tiled=True).reshape(D, w.shape[-1])


def scatter_weight(w):
    return lax.psum_scatter(w.reshape(NW, NT * 16, -1), T_AXES, scatter_dimension=1, tiled=True)


def local(
    tokens, norm_gain, w_query, key_matrix, value_matrix, query_gain, key_gain, w_out, ffn_gain,
    w_gate, w_up, w_down, cotangent,
):
    s = (lax.axis_index("x") * 2 + lax.axis_index("c")) * 2 + lax.axis_index("t")
    state = tokens.astype(f32)
    normal_one, inverse_one = norm_forward(state)
    normalized_input = (normal_one * norm_gain).astype(bf16)
    stage = jnp.concatenate(
        [
            w.reshape(32, 4, -1)
            for w in (w_query, key_matrix, value_matrix, w_out, w_gate, w_up, w_down)
        ],
        axis=2,
    ).transpose(1, 0, 2)
    normed_all, qkv, rest = spread(normalized_input, stage)
    normed_all = normed_all.reshape(TOK, D)
    qkv = qkv.reshape(D, QKV)
    out_w = gather_weight(rest[:, :, :QC])
    gate_up_w = gather_weight(rest[:, :, QC : QC + 2 * FC])
    down_w = gather_weight(rest[:, :, QC + 2 * FC :])

    projected = jnp.dot(normed_all, qkv, preferred_element_type=f32)
    query_pre = projected[:, :QC].reshape(TOK, 2, HD)
    key_pre = projected[:, QC : QC + KC].reshape(TOK, 1, HD)
    value_bf = projected[:, QC + KC :].astype(bf16)
    at = jnp.arange(TOK, dtype=jnp.int32)
    position = (at // ROWS) * (NT * ROWS) + s * ROWS + at % ROWS
    exponent = jnp.arange(0, HD, 2, dtype=f32) / HD
    angles = position.astype(f32)[:, None] * (1.0 / rope_base**exponent)[None, :]
    cosine, sine_table = jnp.cos(angles)[:, None, :], jnp.sin(angles)[:, None, :]
    query_normal, query_inverse = norm_forward(query_pre)
    key_normal, key_inverse = norm_forward(key_pre)
    query_rot = rotate(query_normal * query_gain, cosine, sine_table).astype(bf16)
    key_rot = rotate(key_normal * key_gain, cosine, sine_table).astype(bf16)
    packed = jnp.concatenate([key_rot.reshape(TOK, KC), value_bf], axis=1)
    kv_all, grad_all = gather_keys(packed, cotangent, 1)
    query_rows = to_rows(query_rot)
    raw, sums = attend(query_rows, kv_all)
    total = jnp.sum(sums, axis=1, keepdims=True)
    attended_rows = raw / total
    lse2 = jnp.log2(total).reshape(1, NROW)
    context_bf = from_rows(attended_rows).astype(bf16)
    middle_state = state + sum_rows(cross_rows(context_bf, out_w), 2)
    normal_two, inverse_two = norm_forward(middle_state)
    normed_two = (normal_two * ffn_gain).astype(bf16)
    normed_two_all = gather_rows(normed_two, 3)
    gate_up = jnp.dot(normed_two_all, gate_up_w, preferred_element_type=f32)
    gate_value = gate_up[:, :FC]
    upward = gate_up[:, FC:]
    sigmoid_gate = jax.nn.sigmoid(gate_value)
    activated = gate_value * sigmoid_gate
    hidden = (activated * upward).astype(bf16)
    grad_hidden = jnp.dot(grad_all, down_w, preferred_element_type=f32)
    grad_gate = grad_hidden * upward * (sigmoid_gate * (1.0 + gate_value * (1.0 - sigmoid_gate)))
    grad_upward = grad_hidden * activated
    grad_gate_up = jnp.concatenate([grad_gate, grad_upward], axis=1).astype(bf16)
    grad_normed_two = sum_rows(cross_rows(grad_gate_up, gate_up_w), 4)
    result = (middle_state + sum_rows(cross_rows(hidden, down_w), 5)).astype(bf16)
    ffn_grads = scatter_weight(
        jnp.concatenate(
            [over_tokens(normed_two_all, grad_gate_up), over_tokens(grad_all, hidden)], axis=1
        )
    )
    grad_middle = cotangent.astype(f32) + norm_backward(
        grad_normed_two, normal_two, inverse_two, ffn_gain
    )
    gain_two = jnp.sum(grad_normed_two * normal_two, axis=0)
    grad_middle_all = gather_rows(grad_middle.astype(bf16), 6)
    grad_context = jnp.dot(grad_middle_all, out_w, preferred_element_type=f32).astype(bf16)
    grad_rows = to_rows(grad_context)
    delta = jnp.sum(grad_rows.astype(f32) * attended_rows, axis=1).reshape(1, NROW)
    grad_query_rows, grad_packed = attend_back(query_rows, grad_rows, lse2, delta, kv_all)
    grad_own = sum_keys(grad_packed, 7)
    grad_key_rot = grad_own[:, :KC].reshape(TOK, 1, HD)
    grad_value_bf = grad_own[:, KC:].astype(bf16)
    grad_query_rot = from_rows(grad_query_rows * score_scale).reshape(TOK, 2, HD)
    grad_query_norm = rotate(grad_query_rot, cosine, -sine_table)
    grad_key_norm = rotate(grad_key_rot, cosine, -sine_table)
    gain_query = jnp.sum(grad_query_norm * query_normal, axis=(0, 1))
    gain_key = jnp.sum(grad_key_norm * key_normal, axis=(0, 1))
    grad_query_pre = norm_backward(
        grad_query_norm, query_normal, query_inverse, query_gain
    ).reshape(TOK, QC)
    grad_key_pre = norm_backward(grad_key_norm, key_normal, key_inverse, key_gain).reshape(TOK, KC)
    grad_projected = jnp.concatenate(
        [grad_query_pre.astype(bf16), grad_key_pre.astype(bf16), grad_value_bf], axis=1
    )
    grad_normed = sum_rows(cross_rows(grad_projected, qkv), 8)
    grad_input = grad_middle + norm_backward(grad_normed, normal_one, inverse_one, norm_gain)
    gain_one = jnp.sum(grad_normed * normal_one, axis=0)
    attn_grads = scatter_weight(
        jnp.concatenate(
            [over_tokens(normed_all, grad_projected), over_tokens(grad_middle_all, context_bf)], axis=1
        )
    )
    back = return_weights(jnp.concatenate([attn_grads, ffn_grads], axis=2), 9)
    back = back.reshape(4, 32, COLS).transpose(1, 0, 2).astype(f32)
    cuts = [0]
    for w in (QC, KC, KC, QC, FC, FC, FC):
        cuts.append(cuts[-1] + w)
    grads = [back[:, :, a:b].reshape(32, -1) for a, b in zip(cuts[:-1], cuts[1:])]
    gain_one, gain_two, gain_query, gain_key = lax.psum(
        (gain_one, gain_two, gain_query, gain_key), AXES
    )
    return (
        result, grad_input, gain_one, grads[0], grads[1], grads[2], gain_query, gain_key, grads[3],
        gain_two, grads[4], grads[5], grads[6],
    )


def solution(mesh):
    fine = Mesh(mesh.devices.reshape(4, 2, 4, 2, 2), AXES)
    rows = P(AXES, None)
    weight = P(("z", "yl", "x", "c"), "t")
    return jax.shard_map(
        local,
        mesh=fine,
        in_specs=(rows, P(), weight, weight, weight, P(), P(), weight, P(), weight, weight, weight, rows),
        out_specs=(
            rows, rows, P(), weight, weight, weight, P(), P(), weight, P(), weight, weight, weight,
        ),
        check_vma=False,
    )
```

time: 1930 us -> 630 us (0.33)
  waiting for transfers between devices: 1020 us -> 58 us
  blocking collectives: 630 us -> 75 us
  Pallas kernels: 0 us -> 338 us
  matrix products: 112 us -> 53.3 us
  other arithmetic: 88.1 us -> 37.2 us
    psum x1, blocking collectives: 589 us -> 75 us  [local(): lax.psum((gain_one, gain_two, gain_query, gain_key), AXES)]
    all_gather x5 -> x3, waiting for transfers between devices: 543 us -> 36.6 us  [gather_weight(): return lax.all_gather(w, T_AXES, axis=1, tiled=True).reshape(D, w.shape[-1])]
    reduce_scatter x6 -> x2, waiting for transfers between devices: 471 us -> 21.3 us  [scatter_weight(): lax.psum_scatter(w.reshape(NW, NT * 16, -1), T_AXES, scatter_dimension=1,...]
    pallas_call x0 -> x12, Pallas kernels: none -> 338 us  [the longest x4 95.6 us: sum_rows(): pl.pallas_call(sum_kernel, out_shape=jax.ShapeDtypeStruct((ROWS, D), f32)...]
    concatenate x5 -> x4, other arithmetic: 71 us -> 16.1 us  [the longest x1 11.3 us: local(): jnp.concatenate([over_tokens(normed_two_all, grad_gate_up), over_tokens(g...]
    all_gather x4 -> x0, blocking collectives: 41 us -> none  [gather_rows(): return lax.all_gather(value_rows, 'tp', axis=0, tiled=True)]
    dot_general x4, matrix products: 42.2 us -> 14 us  [over_tokens(): lax.dot_general(left_side, right_side, (((0,), (0,)), ((), ())), preferre...]
  transfers between devices with their start and end apart: 11 -> 5, of which waited for: 8 -> 2; matrix products, arithmetic and copies ran while one was open for 9% -> 12% of each run, Pallas kernels for 0% -> 24%
where the time goes in v1:
time: 630 us; the launch traced here: 619 us
  Pallas kernels  338 us (54%)
  blocking collectives  75 us (12%)
  waiting for transfers between devices  58 us (9%)
  matrix products  53.3 us (8%)
  local copies, waits for them, and re-layouts  43 us (7%)
  other arithmetic  37.2 us (6%)
  between operations  14.9 us (2%)
    pallas_call x4, Pallas kernels, sum_rows(): pl.pallas_call(sum_kernel, out_shape=jax.ShapeDtypeStruct((ROWS, D), f32)...  95.6 us
    psum x1, blocking collectives, local(): lax.psum((gain_one, gain_two, gain_query, gain_key), AXES)  75 us
    pallas_call x1, Pallas kernels, spread(): pl.pallas_call(spread_kernel, out_shape=(jax.ShapeDtypeStruct((NW, ROWS,...  42.7 us
    pallas_call x1, Pallas kernels, sum_keys(): pl.pallas_call(sum_keys_kernel, out_shape=jax.ShapeDtypeStruct((NW, ROWS,...  41.2 us
    pallas_call x2, Pallas kernels, gather_rows(): pl.pallas_call(gather_kernel, out_shape=jax.ShapeDtypeStruct((NW,) + x.sh...  40.7 us
    all_gather x3, waiting for transfers between devices, gather_weight(): return lax.all_gather(w, T_AXES, axis=1, tiled=True).reshape(D, w.shape[-1])  36.6 us
    pallas_call x1, Pallas kernels, gather_keys(): pl.pallas_call(keys_kernel, out_shape=(jax.ShapeDtypeStruct((NW, NT, ROWS...  35 us
    pallas_call x1, Pallas kernels, attend_back(): pl.pallas_call(attend_back_kernel, out_shape=(jax.ShapeDtypeStruct((NROW,...  32.4 us
  transfers between devices with their start and end apart: 5, of which 2 were waited for; matrix products, arithmetic and copies ran while one was open for 12% of the time, Pallas kernels for 24%

profile of v1, /device:TPU:17, one launch (start us, length us, event | category | flops | bytes accessed | tf_op | source)
XLA Modules:
  0.0 619.4 jit_solution(8284881786658519596)
XLA Ops:
  15.5 42.7 %spread.1 = (bf16[8,64,2048]{2,1,0:T(8,128)(2,1)}, bf16[8,16,16,512]{3,2,1,0:T(8,128)(2,1)}, bf16[8,16,2560]{2,1,0:T(8,128)(2,1)}) custom-call(bf16[64,2048]{1,0:T(8,128)(2,1)} %fusion.5.normed_ref, bf16[4,32,3072]{2,1,0:T(8,128)(2,1)} %bitcast.180), custom_call_target="tpu_custom_call" | custom-call | tf_op jit(solution)/shard_map/spread/pallas_call | solution.py:413
  73.0 35.0 %gather_keys.1 = (bf16[8,16,64,256]{3,2,1,0:T(8,128)(2,1)}, bf16[8,64,2048]{2,1,0:T(8,128)(2,1)}) custom-call(bf16[8,64,256]{2,1,0:T(8,128)(2,1)} %pad_maximum_fusion.8.kv_ref, bf16[64,2048]{1,0:T(8,128)(2,1)} %cot_ref.1), custom_call_target="tpu_custom_call" | custom-call | tf_op jit(solution)/shard_map/gather_keys/pallas_call | solution.py:478
  108.0 20.0 %attend.1 = (f32[1024,128]{1,0:T(8,128)}, f32[1024,128]{1,0:T(8,128)}) custom-call(bf16[1024,128]{1,0:T(8,128)(2,1)} %bitcast.158, bf16[8192,256]{1,0:T(8,128)(2,1)} %bitcast.152), custom_call_target="tpu_custom_call" | custom-call | tf_op jit(solution)/shard_map/attend/pallas_call | solution.py:674
  134.7 30.5 %sum_rows.4 = f32[64,2048]{1,0:T(8,128)} custom-call(bf16[8,64,2048]{2,1,0:T(8,128)(2,1)} %bitcast.155), custom_call_target="tpu_custom_call" | custom-call | tf_op jit(solution)/shard_map/sum_rows/pallas_call | solution.py:505
  167.4 20.0 %gather_rows.2 = bf16[8,64,2048]{2,1,0:T(8,128)(2,1)} custom-call(bf16[64,2048]{1,0:T(8,128)(2,1)} %multiply_convert_fusion.3.x_ref), custom_call_target="tpu_custom_call" | custom-call | tf_op jit(solution)/shard_map/gather_rows/pallas_call | solution.py:442
  187.4 8.6 %fusion.55 = f32[512,1536]{1,0:T(8,128)} fusion(bf16[512,2048]{1,0:T(8,128)(2,1)} %bitcast.164, bf16[2048,1536]{1,0:T(8,128)(2,1)} %bitcast.196), kind=kOutput, calls=%fused_computation.145 | convolution fusion | flops 3221225472 | bytes 11534336 | tf_op jit(solution)/shard_map/dot_general | solution.py:837
  196.0 36.5 %all-gather.8.cloned.1.call-done = bf16[8,256,768]{2,1,0:T(8,128)(2,1)} async-done(((bf16[8,16,768]{2,1,0:T(8,128)(2,1)}), bf16[8,256,768]{2,1,0:T(8,128)(2,1)}) %all-gather.8.cloned.1.call-update) | async-done | bytes 3145744 | tf_op jit(solution)/shard_map/all_gather | solution.py:783
  232.6 6.6 %multiply_convert_fusion.1 = (bf16[512,768]{1,0:T(8,128)(2,1)S(1)}, bf16[512,768]{1,0:T(8,128)(2,1)S(1)}, bf16[512,768]{1,0:T(8,128)(2,1)}) fusion(f32[512,1536]{1,0:T(8,128)} %fusion.55, bf16[512,2048]{1,0:T(8,128)(2,1)} %bitcast.204, bf16[2048,768]{1,0:T(8,128)(2,1)} %bitcast.198), kind=kOutput, calls=%fused_computation.13 | convolution fusion | flops 1616510976 | bytes 10747904 | tf_op jit(solution)/shard_map/dot_general | solution.py:843
  239.2 4.7 convolution_convert_fusion.5
  243.9 21.3 %sum_rows.6 = f32[64,2048]{1,0:T(8,128)} custom-call(bf16[8,64,2048]{2,1,0:T(8,128)(2,1)} %bitcast.163), custom_call_target="tpu_custom_call" | custom-call | tf_op jit(solution)/shard_map/sum_rows/pallas_call | solution.py:505
  268.5 20.7 %gather_rows.3 = bf16[8,64,2048]{2,1,0:T(8,128)(2,1)} custom-call(bf16[64,2048]{1,0:T(8,128)(2,1)} %fusion.53.x_ref), custom_call_target="tpu_custom_call" | custom-call | tf_op jit(solution)/shard_map/gather_rows/pallas_call | solution.py:442
  296.3 32.4 %attend_back.1 = (f32[1024,128]{1,0:T(8,128)}, bf16[8192,256]{1,0:T(8,128)(2,1)}) custom-call(bf16[1024,128]{1,0:T(8,128)(2,1)} %bitcast.159, bf16[1024,128]{1,0:T(8,128)(2,1)} %bitcast.160, f32[1,1024]{1,0:T(1,128)} %bitcast.195, f32[1,1024]{1,0:T(1,128)} %bitcast.194, bf16[8192,256]{1,0:T(8,128)(2,1)} %bitcast.153), custom_call_target="tpu_custom_call" | custom-call | tf_op jit(solution)/shard_map/attend_back/pallas_call | solution.py:726
  328.7 41.2 %sum_keys.1 = f32[8,64,256]{2,1,0:T(8,128)} custom-call(bf16[8,4,2,2,64,256]{5,4,3,2,1,0:T(8,128)(2,1)} %bitcast.157), custom_call_target="tpu_custom_call" | custom-call | tf_op jit(solution)/shard_map/sum_keys/pallas_call | solution.py:555
  384.8 4.7 copy.92
  394.3 4.1 convolution_convert_fusion
  398.3 11.3 %pad_maximum_fusion = bf16[2048,2304]{0,1:T(8,128)(2,1)} fusion(bf16[2048,768]{0,1:T(8,128)(2,1)S(1)} %convolution_convert_fusion.1, bf16[2048,1536]{0,1:T(8,128)(2,1)S(1)} %convolution_convert_fusion), kind=kLoop, calls=%fused_computation | loop fusion | flops 18874368 | bytes 18874368 | tf_op jit(solution)/shard_map/concatenate | solution.py:850
  409.7 12.7 %copy.93 = bf16[2048,2304]{1,0:T(8,128)(2,1)} copy(bf16[2048,2304]{0,1:T(8,128)(2,1)} %pad_maximum_fusion) | data formatting | bytes 18874368 | tf_op jit(solution)/shard_map/concatenate | solution.py:850
  422.4 4.2 convolution_convert_fusion.4
  426.7 22.9 %sum_rows.7 = f32[64,2048]{1,0:T(8,128)} custom-call(bf16[8,64,2048]{2,1,0:T(8,128)(2,1)} %bitcast.161), custom_call_target="tpu_custom_call" | custom-call | tf_op jit(solution)/shard_map/sum_rows/pallas_call | solution.py:505
  449.6 5.0 convolution_convert_fusion.6
  454.6 20.8 %sum_rows.5 = f32[64,2048]{1,0:T(8,128)} custom-call(bf16[8,64,2048]{2,1,0:T(8,128)(2,1)} %bitcast.162), custom_call_target="tpu_custom_call" | custom-call | tf_op jit(solution)/shard_map/sum_rows/pallas_call | solution.py:505
  475.7 75.0 %all-reduce = (f32[2048]{0:T(1024)}, f32[128]{0:T(128)}, f32[128]{0:T(128)}, f32[2048]{0:T(1024)}) all-reduce(f32[2048]{0:T(1024)S(1)} %get-tuple-element.35, f32[128]{0:T(128)S(1)} %bitcast_reduce_fusion, f32[128]{0:T(128)S(1)} %get-tuple-element.31, ...), channel_id=1, replica_groups=mesh['z'=4,'yl'=2,'x'=4,'c'=2,'t'=2] {'z','yl','x','c','t'}, use_global_device_ids=true, to_apply=%region_11.12 | all-reduce | flops 4352 | bytes 34816 | tf_op jit(solution)/shard_map/psum | solution.py:892
  552.9 21.3 %reduce-scatter.5.cloned.1.call-done = bf16[8,16,2304]{2,1,0:T(8,128)(2,1)} async-done(((bf16[8,256,2304]{2,1,0:T(8,128)(2,1)}), bf16[8,16,2304]{2,1,0:T(8,128)(2,1)}) %reduce-scatter.5.cloned.1.call-update) | async-done | bytes 589840 | tf_op jit(solution)/shard_map/reduce_scatter | solution.py:787
  576.3 30.3 %return_weights.1 = bf16[4,2,16,3072]{3,2,1,0:T(8,128)(2,1)} custom-call(bf16[8,16,3072]{2,1,0:T(8,128)(2,1)} %pad_maximum_fusion.5.x_ref), custom_call_target="tpu_custom_call" | custom-call | tf_op jit(solution)/shard_map/return_weights/pallas_call | solution.py:627
  (151 shorter events, 71.8 us)
Async XLA Ops:
  7.2 3.9 copy-start
  7.2 7.4 %copy-start.15 = (bf16[32,3072]{1,0:T(8,128)(2,1)S(1)}, bf16[32,3072]{1,0:T(8,128)(2,1)}, u32[]{:S(2)}) copy-start(bf16[32,3072]{1,0:T(8,128)(2,1)} %param.24) | copy-start | bytes 589828
  7.2 124.2 %all-gather.4.cloned.1.call-start = ((), (), s32[]{:S(2)}) async-start(), calls=%async_computation.2 | async-start | bytes 1114112 | tf_op jit(solution)/shard_map/all_gather | solution.py:783
  59.7 127.7 %all-gather.6.cloned.1.call-start = ((), (), s32[]{:S(2)}) async-start(), calls=%async_computation.3 | async-start | bytes 6684672 | tf_op jit(solution)/shard_map/all_gather | solution.py:783
  61.5 171.0 %all-gather.8.cloned.1.call-start = ((), (), s32[]{:S(2)}) async-start(), calls=%async_computation.4 | async-start | bytes 3342336 | tf_op jit(solution)/shard_map/all_gather | solution.py:783
  63.2 489.7 %reduce-scatter.3.cloned.1.call-start = ((), (), s32[]{:S(2)}) async-start(), calls=%async_computation.5 | async-start | bytes 3342336 | tf_op jit(solution)/shard_map/reduce_scatter | solution.py:787
  134.7 30.6 %copy-start.3 = (bf16[64,2048]{1,0:T(8,128)(2,1)S(1)}, bf16[64,2048]{1,0:T(8,128)(2,1)}, u32[]{:S(2)}) copy-start(bf16[64,2048]{1,0:T(8,128)(2,1)} %param.13) | copy-start | bytes 786436
  134.7 31.8 %copy-start.16 = (f32[2048]{0:T(1024)S(1)}, f32[2048]{0:T(1024)}, u32[]{:S(2)}) copy-start(f32[2048]{0:T(1024)} %param.21) | copy-start | bytes 24580
  232.6 6.6 %copy-start.20 = (bf16[8,256,1536]{2,1,0:T(8,128)(2,1)S(1)}, bf16[8,256,1536]{2,1,0:T(8,128)(2,1)}, u32[]{:S(2)}) copy-start(bf16[8,256,1536]{2,1,0:T(8,128)(2,1)} %all-gather.6.cloned.1.call-done) | copy-start | bytes 18874372
  239.2 4.7 copy-start.22
  239.2 4.7 copy-start.24
  243.9 22.7 %copy-start.6 = (bf16[64,2048]{1,0:T(8,128)(2,1)S(1)}, bf16[64,2048]{1,0:T(8,128)(2,1)}, u32[]{:S(2)}) copy-start(bf16[64,2048]{1,0:T(8,128)(2,1)} %cot_ref.1) | copy-start | bytes 786436
  289.2 6.1 copy-start.8
  328.7 43.8 %copy-start.12 = (bf16[8,2,64,128]{3,1,2,0:T(2,128)(2,1)S(1)}, bf16[8,2,64,128]{3,1,2,0:T(2,128)(2,1)}, u32[]{:S(2)}) copy-start(bf16[8,2,64,128]{3,1,2,0:T(2,128)(2,1)} %copy-done.11) | copy-start | bytes 786436
  372.4 3.4 copy-start.14
  380.0 3.0 copy-start.10
  389.5 184.7 %reduce-scatter.5.cloned.1.call-start = ((), (), s32[]{:S(2)}) async-start(), calls=%async_computation.6 | async-start | bytes 10027008 | tf_op jit(solution)/shard_map/reduce_scatter | solution.py:787
  390.6 3.6 copy-start.7
  390.6 3.6 copy-start.23
  390.6 3.6 copy-start.25
  454.6 20.8 %copy-start.4 = (f32[64,2048]{1,0:T(8,128)S(1)}, f32[64,2048]{1,0:T(8,128)}, u32[]{:S(2)}) copy-start(f32[64,2048]{1,0:T(8,128)} %sum_rows.7) | copy-start | bytes 1572868
  454.6 20.8 %copy-start.17 = (f32[2048]{0:T(1024)S(1)}, f32[2048]{0:T(1024)}, u32[]{:S(2)}) copy-start(f32[2048]{0:T(1024)} %param.14) | copy-start | bytes 24580
  454.6 96.0 %copy-start.2 = (f32[64,2048]{1,0:T(8,128)S(1)}, f32[64,2048]{1,0:T(8,128)}, u32[]{:S(2)}) copy-start(f32[64,2048]{1,0:T(8,128)} %sum_rows.6) | copy-start | bytes 1572868
  607.9 4.5 copy-start.1
  (7 other events, 8.4 us)
Sparse Core Ops, SparseCore 0:
  59.8 44.1 all-gather.3
  107.2 74.0 all-gather.5
  183.8 48.6 all-gather.7
  389.7 73.9 reduce-scatter.2
  468.0 106.2 reduce-scatter.4

commit v2 on v1

--- a/solution.py
+++ b/solution.py
@@ -22,6 +22,9 @@
 QKV = QC + 2 * KC
 COLS = QKV + QC + 3 * FC
 VMEM_LIMIT = 60 << 20
+KB = 256
+CH = 2 * ROWS
+NROW = NW * CH
 
 epsilon = 1e-06
 rope_base = 1000000.0
@@ -180,13 +183,16 @@
         rows = self.slot(kind)
         self.part[g, lo:hi] = (self.part[g, lo:hi].astype(f32) + rows[...].astype(f32)).astype(bf16)
 
-    def run(self):
+    def leaf(self):
         dp, dm, dy = self.dp, self.dm, self.dy
         self.put(0, self.goo, 32, 64, dy)
         self.put(3, self.goo, 16, 32, dm)
         self.put(4, self.goo, 0, 16, dp)
         self.put(1, self.gmo, 32, 64, dy)
         self.put(2, self.gpo, 32, 64, dy)
+
+    def two(self):
+        dp, dm, dy = self.dp, self.dm, self.dy
         self.got(0, dy)
         self.add(0, self.go, 32, 64)
         self.put(5, self.go, 16, 48, dm)
@@ -198,6 +204,9 @@
         self.got(4, dm)
         self.add(4, self.gpo, 0, 16)
         self.put(8, self.gpo, 0, 32, dp)
+
+    def three(self):
+        dp, dm, dy = self.dp, self.dm, self.dy
         self.got(1, dy)
         self.add(1, self.gm, 32, 64)
         self.got(5, dp)
@@ -207,20 +216,31 @@
         self.add(2, self.gp, 32, 64)
         self.s.recv(6, self.slot(6, 0, 16), dm)
         self.s.recv(11, self.slot(6, 16, 16), dm)
-        lo, hi = self.slot(6, 0, 16), self.slot(6, 16, 16)
-        self.part[self.gp, 0:16] = (self.part[self.gp, 0:16].astype(f32) + lo[...].astype(f32)).astype(bf16)
-        self.part[self.gp, 48:64] = (self.part[self.gp, 48:64].astype(f32) + hi[...].astype(f32)).astype(bf16)
+        for lo, hi, at in ((0, 16, 0), (48, 64, 16)):
+            rows = self.slot(6, at, 16)
+            self.part[self.gp, lo:hi] = (
+                self.part[self.gp, lo:hi].astype(f32) + rows[...].astype(f32)
+            ).astype(bf16)
         self.put(10, self.gp, 0, 64, dp)
         self.got(7, dp)
         self.add(7, self.own_o, 0, 32)
         self.got(8, dm)
         self.add(8, self.own_o, 0, 32)
         self.s.send(12, self.part.at[self.own_o], self.slot(11), dy)
+
+    def total(self):
+        dp, dm, dy = self.dp, self.dm, self.dy
         self.got(9, dp)
         self.got(10, dm)
         self.s.recv(12, self.slot(11), dy)
         total = self.part[self.own].astype(f32) + self.slot(9)[...].astype(f32)
         return total + self.slot(10)[...].astype(f32) + self.slot(11)[...].astype(f32)
+
+    def run(self):
+        self.leaf()
+        self.two()
+        self.three()
+        return self.total()
 
 
 SUMW_ROWS = sum(SumW.LAND)
@@ -313,7 +333,41 @@
     return [DMA((n,)), DMA((n,))]
 
 
-def spread_kernel(normed_ref, stage_ref, normed_all, weights, rest, ssem, rsem, local):
+GROUPS = (QKV, QC, 2 * FC, FC)
+STARTS = (0, QKV, QKV + QC, QKV + QC + 2 * FC)
+PARTIAL = 3 * FC
+
+
+def rms(v):
+    return lax.rsqrt(jnp.mean(v * v, axis=-1, keepdims=True) + epsilon)
+
+
+def mul_rows(a, b):
+    return lax.dot_general(a, b, (((1,), (1,)), ((), ())), preferred_element_type=f32)
+
+
+def mul(a, b):
+    return jnp.dot(a, b, preferred_element_type=f32)
+
+
+def mul_tokens(a, b):
+    return lax.dot_general(a, b, (((0,), (0,)), ((), ())), preferred_element_type=f32)
+
+
+def row_sums(v):
+    ones = jnp.ones((8, v.shape[1]), f32)
+    return lax.dot_general(
+        ones, v, (((1,), (1,)), ((), ())), preferred_element_type=f32, precision=lax.Precision.HIGHEST
+    )[0:1]
+
+
+def forward_kernel(
+    tok, cot, ngain, fgain, qgain, kgain, cosr, sinr, wq, wk, wv, wo, wg, wu, wd,
+    middle, grad_mid, gain_two, q_rows, do_rows, lse, delta, qk_pre, ctx, part_two, gm_all,
+    kv_out, qkv_out, normed_out, partial,
+    stage, normed_all, cot_all, nt_all, kv_all, wqkv, wout, wgu, wdn, part, land, o_acc, l_acc,
+    gate, up, gh, hidden, dgu, buf, ssem, rsem, lsem,
+):
     me = place()
     z, y, t = me["z"], me["yl"], me["t"]
     own_g = 2 * z + y
@@ -332,162 +386,305 @@
                     )
     for d in t_devices(me)[:2] + t_devices(me)[3:]:
         pl.semaphore_signal(sem, inc=1, device_id=d, device_id_type=MESH)
+
+    state = tok[...].astype(f32)
+    normed_all[own_g] = (state * rms(state) * ngain[...]).astype(bf16)
+    cot_all[own_g] = cot[...]
+    at = 0
+    for w in (wq, wk, wv, wo, wg, wu, wd):
+        n = w.shape[1] // 4
+        for j in range(4):
+            stage[j, :, at : at + n] = w[:, j * n : (j + 1) * n]
+        at += n
     pl.semaphore_wait(sem, 18)
 
-    mine = pltpu.make_async_copy(normed_ref, normed_all.at[own_g], local.at[0])
-    mine.start()
-    base_b = GatherW.KINDS
-    base_c = base_b + 8
-    for j in range(4):
-        for t2 in range(2):
-            g = 4 * t + j
-            dst_z, dst_y = 2 * t + j // 2, j % 2
-            is_me = (dst_z == z) & (dst_y == y) & (t == t2)
-            src = stage_ref.at[j, 16 * t2 : 16 * t2 + 16]
-            to = {"z": dst_z, "yl": dst_y, "t": jnp.int32(t2)}
-            qk = remote(
-                src.at[:, :QKV], weights.at[own_g, s - t + t2], ssem.at[base_b + j * 2 + t2],
-                rsem.at[base_b + own_g], to,
-            )
-            ot = remote(
-                src.at[:, QKV:], rest.at[own_g], ssem.at[base_c + j * 2 + t2], rsem.at[base_c + own_g], to,
-            )
-            lq = pltpu.make_async_copy(src.at[:, :QKV], weights.at[own_g, s], local.at[1])
-            lo = pltpu.make_async_copy(src.at[:, QKV:], rest.at[own_g], local.at[2])
-
-            @pl.when(is_me)
+    count = [0]
+
+    def sends(n):
+        base = count[0]
+        count[0] += n
+        return Sends(ssem, rsem, base)
+
+    gw = GatherW(me, normed_all, sends(GatherW.KINDS))
+    gw.start()
+
+    full = (wqkv, wout, wgu, wdn)
+    base = count[0]
+    count[0] += 32
+    holder = own_g // 4
+
+    def to_holders(groups):
+        for j in range(4):
+            for t2 in range(2):
+                dst_z, dst_y = 2 * t + j // 2, j % 2
+                is_me = (dst_z == z) & (dst_y == y) & (t == t2)
+                src = stage.at[j, 16 * t2 : 16 * t2 + 16]
+                to = {"z": dst_z, "yl": dst_y, "t": jnp.int32(t2)}
+                remotes, locals_ = [], []
+                for k in groups:
+                    piece = src.at[:, STARTS[k] : STARTS[k] + GROUPS[k]]
+                    remotes.append(
+                        remote(
+                            piece, full[k].at[own_g, s - t + t2], ssem.at[base + 8 * k + 2 * j + t2],
+                            rsem.at[base + 8 * k + own_g], to,
+                        )
+                    )
+                    locals_.append(pltpu.make_async_copy(piece, full[k].at[own_g, s], lsem.at[k]))
+
+                @pl.when(is_me)
+                def _():
+                    for c in locals_:
+                        c.start()
+                    for c in locals_:
+                        c.wait()
+
+                @pl.when(jnp.logical_not(is_me))
+                def _():
+                    for c in remotes:
+                        c.start()
+
+    def from_owners(groups):
+        for g in range(8):
+            from_me = (own_g == g) & (holder == t)
+
+            @pl.when(jnp.logical_not(from_me))
+            def _(g=g):
+                for k in groups:
+                    dst = full[k].at[g, s]
+                    remote(dst, dst, ssem.at[0], rsem.at[base + 8 * k + g], dy).wait_recv()
+
+    to_holders((0,))
+    from_owners((0,))
+    gq, go, gg, gd = [GatherT(me, w, sends(GatherT.KINDS)) for w in full]
+    gq.start()
+    gw.middle()
+    to_holders((1, 2, 3))
+    gq.middle()
+    gw.end()
+    gq.end()
+
+    keep = [
+        pltpu.make_async_copy(wqkv, qkv_out, lsem.at[4]),
+        pltpu.make_async_copy(normed_all, normed_out, lsem.at[5]),
+    ]
+    for c in keep:
+        c.start()
+
+    for h in range(2):
+        rows = slice(h * 256, h * 256 + 256)
+        pre = mul(
+            normed_all[4 * h : 4 * h + 4].reshape(256, D), wqkv[...].reshape(D, QKV)
+        )
+        qk_pre[rows] = pre[:, : QC + KC]
+        cosine, sine = cosr[rows], sinr[rows]
+        for head in range(3):
+            u = pre[:, head * HD : head * HD + HD]
+            n = u * rms(u) * (qgain if head < 2 else kgain)[...]
+            rolled = jnp.concatenate([n[:, HD // 2 :], n[:, : HD // 2]], axis=1)
+            rot = (n * cosine + rolled * sine).astype(bf16)
+            for i in range(4):
+                g = 4 * h + i
+                piece = rot[i * ROWS : i * ROWS + ROWS]
+                if head < 2:
+                    q_rows[g * CH + head * ROWS : g * CH + head * ROWS + ROWS] = piece
+                else:
+                    kv_all[g, s, :, :KC] = piece
+        val = pre[:, QC + KC :].astype(bf16)
+        for i in range(4):
+            kv_all[4 * h + i, s, :, KC:] = val[i * ROWS : i * ROWS + ROWS]
+
+    gk = GatherT(me, kv_all, sends(GatherT.KINDS))
+    gc = GatherW(me, cot_all, sends(GatherW.KINDS))
+    gk.start()
+    gc.start()
+    from_owners((1, 2, 3))
+    go.start()
+    gg.start()
+    gk.middle()
+    gc.middle()
+    gk.end()
+    keep.append(pltpu.make_async_copy(kv_all, kv_out, lsem.at[6]))
+    keep[-1].start()
+
+    o_acc[...] = jnp.zeros_like(o_acc)
+    l_acc[...] = jnp.zeros_like(l_acc)
+    attend_blocks(range(0, 2), s, q_rows, kv_all, o_acc, l_acc)
+    go.middle()
+    gg.middle()
+    gc.end()
+    gd.start()
+    attend_blocks(range(2, 8), s, q_rows, kv_all, o_acc, l_acc)
+    go.end()
+    gg.end()
+    gd.middle()
+
+    lse[...] = jnp.log2(row_sums(l_acc[...]))
+    for g in range(NW):
+        rows = slice(g * CH, g * CH + CH)
+        o = o_acc[rows] / jnp.sum(l_acc[rows], axis=1, keepdims=True)
+        o_acc[rows] = o
+        ctx[g * ROWS : g * ROWS + ROWS, :HD] = o[:ROWS].astype(bf16)
+        ctx[g * ROWS : g * ROWS + ROWS, HD:] = o[ROWS:].astype(bf16)
+    for n in range(4):
+        w = wout[2 * n : 2 * n + 2].reshape(512, QC)
+        part[:, :, n * 512 : n * 512 + 512] = (
+            mul_rows(ctx[...], w).astype(bf16).reshape(NW, ROWS, 512)
+        )
+    sw = SumW(me, part, land, sends(SUMW_SEMS))
+    sw.leaf()
+    sw.two()
+    gd.end()
+    for n in range(3):
+        gh[:, n * 256 : n * 256 + 256] = mul(
+            cot_all[...].reshape(TOK, D), wdn[:, :, :, n * 256 : n * 256 + 256].reshape(D, 256)
+        )
+    sw.three()
+    mid = state + sw.total()
+    middle[...] = mid
+    nt_all[own_g] = (mid * rms(mid) * fgain[...]).astype(bf16)
+    gn = GatherW(me, nt_all, sends(GatherW.KINDS))
+    gn.start()
+    gn.middle()
+    gn.end()
+
+    for n in range(3):
+        cols = slice(n * 256, n * 256 + 256)
+        nt = nt_all[...].reshape(TOK, D)
+        gate[:, cols] = mul(nt, wgu[:, :, :, n * 256 : n * 256 + 256].reshape(D, 256))
+        up[:, cols] = mul(nt, wgu[:, :, :, FC + n * 256 : FC + n * 256 + 256].reshape(D, 256))
+
+    def units(i, carry):
+        rows = pl.ds(pl.multiple_of(i * 64, 64), 64)
+        gv, uv, hv = gate[rows], up[rows], gh[rows]
+        sig = jax.nn.sigmoid(gv)
+        act = gv * sig
+        hidden[rows] = (act * uv).astype(bf16)
+        dgu[rows, :FC] = (hv * uv * (sig * (1.0 + gv * (1.0 - sig)))).astype(bf16)
+        dgu[rows, FC:] = (hv * act).astype(bf16)
+        return carry
+
+    lax.fori_loop(0, TOK // 64, units, 0)
+    sw.s.close()
+    for n in range(4):
+        w = wgu[2 * n : 2 * n + 2].reshape(512, 2 * FC)
+        part[:, :, n * 512 : n * 512 + 512] = (
+            mul_rows(dgu[...], w).astype(bf16).reshape(NW, ROWS, 512)
+        )
+    sb = SumW(me, part, land, sends(SUMW_SEMS))
+    sb.leaf()
+    for n in range(4):
+        w = wdn[2 * n : 2 * n + 2].reshape(512, FC)
+        part_two[:, :, n * 512 : n * 512 + 512] = (
+            mul_rows(hidden[...], w).astype(bf16).reshape(NW, ROWS, 512)
+        )
+    sb.two()
+
+    def weight_grads(lo, hi):
+        def step(g, carry):
+            slot = lax.rem(g, 2)
+
+            @pl.when(g >= 2)
             def _():
-                lq.start()
-                lo.start()
-                lq.wait()
-                lo.wait()
-
-            @pl.when(jnp.logical_not(is_me))
-            def _():
-                qk.start()
-                ot.start()
-
-    mine.wait()
-    gw = GatherW(me, normed_all, Sends(ssem, rsem))
-    gw.start()
-    holder = own_g // 4
-    for g in range(8):
-        from_me = (own_g == g) & (holder == t)
-
-        @pl.when(jnp.logical_not(from_me))
-        def _(g=g):
-            dst = weights.at[g, s]
-            remote(dst, dst, ssem.at[0], rsem.at[base_b + g], dy).wait_recv()
-
-    gt = GatherT(me, weights, Sends(ssem, rsem, base_c + 8))
-    gt.start()
-    gw.middle()
-    gt.middle()
-    gw.end()
-    gt.end()
-    for g in range(8):
-        from_me = (own_g == g) & (holder == t)
-
-        @pl.when(jnp.logical_not(from_me))
-        def _(g=g):
-            dst = rest.at[g]
-            remote(dst, dst, ssem.at[0], rsem.at[base_c + g], dy).wait_recv()
-
+                pltpu.make_async_copy(buf.at[slot], partial.at[g - 2], lsem.at[7 + slot]).wait()
+
+            cols = pl.ds(pl.multiple_of(g * 256, 256), 256)
+            a = nt_all[:, :, cols].reshape(TOK, 256)
+            for n in range(3):
+                c = slice(n * 512, n * 512 + 512)
+                buf[slot, :, c] = mul_tokens(a, dgu[:, c]).astype(bf16)
+            b = cot_all[:, :, cols].reshape(TOK, 256)
+            for n in range(3):
+                c = slice(n * 256, n * 256 + 256)
+                buf[slot, :, 2 * FC + n * 256 : 2 * FC + n * 256 + 256] = mul_tokens(
+                    b, hidden[:, c]
+                ).astype(bf16)
+            pltpu.make_async_copy(buf.at[slot], partial.at[g], lsem.at[7 + slot]).start()
+            return carry
+
+        lax.fori_loop(lo, hi, step, 0)
+
+    weight_grads(0, 2)
+    sb.three()
+    weight_grads(2, 4)
+    gnt = sb.total()
+    mid = middle[...]
+    inv = rms(mid)
+    normal = mid * inv
+    gain_two[...] = jnp.sum(gnt * normal, axis=0, keepdims=True)
+    scaled = gnt * fgain[...]
+    gm = cot[...].astype(f32) + inv * (
+        scaled - normal * jnp.mean(scaled * normal, axis=-1, keepdims=True)
+    )
+    grad_mid[...] = gm
+    gm_all[own_g] = gm.astype(bf16)
+    ga = GatherW(me, gm_all, sends(GatherW.KINDS))
+    ga.start()
+    weight_grads(4, 6)
+    ga.middle()
+    weight_grads(6, 8)
+    ga.end()
+    grad_ctx = mul(gm_all[...].reshape(TOK, D), wout[...].reshape(D, QC)).astype(bf16)
+    for g in range(NW):
+        for head in range(2):
+            do_rows[g * CH + head * ROWS : g * CH + head * ROWS + ROWS] = grad_ctx[
+                g * ROWS : g * ROWS + ROWS, head * HD : head * HD + HD
+            ]
+    delta[...] = row_sums(do_rows[...].astype(f32) * o_acc[...])
+
+    for c in keep:
+        c.wait()
+    for slot in range(2):
+        pltpu.make_async_copy(buf.at[slot], partial.at[6 + slot], lsem.at[7 + slot]).wait()
     for j in range(4):
         for t2 in range(2):
             is_me = (2 * t + j // 2 == z) & (j % 2 == y) & (t == t2)
 
             @pl.when(jnp.logical_not(is_me))
             def _(j=j, t2=t2):
-                src = stage_ref.at[j, 16 * t2 : 16 * t2 + 16]
-                k = j * 2 + t2
-                remote(src.at[:, :QKV], src.at[:, :QKV], ssem.at[base_b + k], rsem.at[0], dy).wait_send()
-                remote(src.at[:, QKV:], src.at[:, QKV:], ssem.at[base_c + k], rsem.at[0], dy).wait_send()
-
-    gw.s.close()
-    gt.s.close()
-
-
-def spread(normed, stage):
-    n = GatherW.KINDS + 16 + GatherT.KINDS
+                src = stage.at[j, 16 * t2 : 16 * t2 + 16]
+                for k in range(4):
+                    piece = src.at[:, STARTS[k] : STARTS[k] + GROUPS[k]]
+                    remote(
+                        piece, piece, ssem.at[base + 8 * k + 2 * j + t2], rsem.at[0], dy
+                    ).wait_send()
+    for g in (gw, gq, go, gg, gd, gk, gc, gn, sb, ga):
+        g.s.close()
+    assert count[0] == FORWARD_SEMS, count[0]
+
+
+FORWARD_SEMS = 4 * GatherW.KINDS + 5 * GatherT.KINDS + 2 * SUMW_SEMS + 32
+
+
+def forward(tok, cot, ngain, fgain, qgain, kgain, cosr, sinr, *weights):
+    def out(shape, dtype):
+        return jax.ShapeDtypeStruct(shape, dtype)
+
+    def vmem(shape, dtype=bf16):
+        return pltpu.VMEM(shape, dtype)
+
     return pl.pallas_call(
-        spread_kernel,
+        forward_kernel,
         out_shape=(
-            jax.ShapeDtypeStruct((NW, ROWS, D), bf16),
-            jax.ShapeDtypeStruct((NW, NT, 16, QKV), bf16),
-            jax.ShapeDtypeStruct((NW, 16, COLS - QKV), bf16),
+            out((ROWS, D), f32), out((ROWS, D), f32), out((1, D), f32), out((NROW, HD), bf16), out((NROW, HD), bf16),
+            out((1, NROW), f32), out((1, NROW), f32), out((TOK, QC + KC), f32), out((TOK, QC), bf16),
+            out((NW, ROWS, D), bf16), out((NW, ROWS, D), bf16),
+            out((NW, NT, ROWS, 2 * KC), bf16), out((NW, NT, 16, QKV), bf16), out((NW, ROWS, D), bf16),
+            out((NW, 256, PARTIAL), bf16),
         ),
-        in_specs=[VM, VM],
-        out_specs=(VM, VM, VM),
-        scratch_shapes=sems(n) + [DMA((3,))],
+        in_specs=[VM] * 15,
+        out_specs=(VM,) * 11 + (ANY,) * 4,
+        scratch_shapes=[
+            vmem((4, 32, COLS)), vmem((NW, ROWS, D)), vmem((NW, ROWS, D)), vmem((NW, ROWS, D)),
+            vmem((NW, NT, ROWS, 2 * KC)), vmem((NW, NT, 16, QKV)), vmem((NW, NT, 16, QC)),
+            vmem((NW, NT, 16, 2 * FC)), vmem((NW, NT, 16, FC)), vmem((NW, ROWS, D)),
+            vmem((SUMW_ROWS, D)), vmem((NROW, HD), f32), vmem((NROW, HD), f32),
+            vmem((TOK, FC), f32), vmem((TOK, FC), f32), vmem((TOK, FC), f32), vmem((TOK, FC)),
+            vmem((TOK, 2 * FC)), vmem((2, 256, PARTIAL)),
+        ]
+        + sems(FORWARD_SEMS) + [DMA((9,))],
         compiler_params=params(0),
-        name="spread",
-    )(normed, stage)
-
-
-def gather_kernel(x_ref, out, ssem, rsem, local):
-    me = place()
-    barrier(w_devices(me))
-    mine = pltpu.make_async_copy(x_ref, out.at[2 * me["z"] + me["yl"]], local)
-    mine.start()
-    mine.wait()
-    g = GatherW(me, out, Sends(ssem, rsem))
-    g.start()
-    g.middle()
-    g.end()
-    g.s.close()
-
-
-def gather_rows(x, cid):
-    out = pl.pallas_call(
-        gather_kernel,
-        out_shape=jax.ShapeDtypeStruct((NW,) + x.shape, x.dtype),
-        in_specs=[VM],
-        out_specs=VM,
-        scratch_shapes=sems(GatherW.KINDS) + [DMA(())],
-        compiler_params=params(cid),
-        name="gather_rows",
-    )(x)
-    return out.reshape(TOK, x.shape[1])
-
-
-def keys_kernel(kv_ref, cot_ref, kv_all, cot_all, ssem, rsem, local):
-    me = place()
-    barrier(t_devices(me) + w_devices(me))
-    s = (me["x"] * 2 + me["c"]) * 2 + me["t"]
-    a = pltpu.make_async_copy(kv_ref, kv_all.at[:, s], local.at[0])
-    b = pltpu.make_async_copy(cot_ref, cot_all.at[2 * me["z"] + me["yl"]], local.at[1])
-    a.start()
-    b.start()
-    a.wait()
-    b.wait()
-    gt = GatherT(me, kv_all, Sends(ssem, rsem))
-    gw = GatherW(me, cot_all, Sends(ssem, rsem, GatherT.KINDS))
-    gt.start()
-    gw.start()
-    gt.middle()
-    gw.middle()
-    gt.end()
-    gw.end()
-    gt.s.close()
-    gw.s.close()
-
-
-def gather_keys(kv, cot, cid):
-    n = GatherT.KINDS + GatherW.KINDS
-    kv_all, cot_all = pl.pallas_call(
-        keys_kernel,
-        out_shape=(
-            jax.ShapeDtypeStruct((NW, NT, ROWS, 2 * KC), bf16),
-            jax.ShapeDtypeStruct((NW, ROWS, D), bf16),
-        ),
-        in_specs=[VM, VM],
-        out_specs=(VM, VM),
-        scratch_shapes=sems(n) + [DMA((2,))],
-        compiler_params=params(cid),
-        name="gather_keys",
-    )(kv.reshape(NW, ROWS, 2 * KC), cot)
-    return kv_all.reshape(SEQ, 2 * KC), cot_all.reshape(TOK, D)
+        name="forward",
+    )(tok, cot, ngain, fgain, qgain, kgain, cosr, sinr, *weights)
 
 
 def sum_kernel(x_ref, out, part, land, ssem, rsem, local):
@@ -635,28 +832,17 @@
     )(x)
 
 
-KB = 256
-CH = 2 * ROWS
-NROW = NW * CH
-
-
-def attend_kernel(q_ref, kv_ref, o_ref, l_ref):
-    s = (lax.axis_index("x") * 2 + lax.axis_index("c")) * 2 + lax.axis_index("t")
-    o_ref[...] = jnp.zeros_like(o_ref)
-    l_ref[...] = jnp.zeros_like(l_ref)
+def attend_blocks(slabs, s, q_ref, kv_ref, o_ref, l_ref):
     factor = score_scale * LOG2E
-    for g in range(NW):
+    for g in slabs:
         first = g * CH
 
         def block(b, carry, g=g, first=first):
-            keys = pl.ds(pl.multiple_of(g * 1024 + b * KB, KB), KB)
-            k = kv_ref[keys, :KC]
-            v = kv_ref[keys, KC:]
+            pair = kv_ref[g, pl.ds(b * 4, 4)].reshape(KB, 2 * KC)
+            k, v = pair[:, :KC], pair[:, KC:]
             for r0 in range(first, NROW, 256):
                 r1 = min(r0 + 256, NROW)
-                sc = lax.dot_general(
-                    q_ref[r0:r1], k, (((1,), (1,)), ((), ())), preferred_element_type=f32
-                )
+                sc = mul_rows(q_ref[r0:r1], k)
                 p = jnp.exp2(sc * factor)
                 if r0 == first:
                     row = lax.broadcasted_iota(jnp.int32, (r1 - r0, KB), 0)
@@ -664,24 +850,10 @@
                     seen = (row >= CH) | (s * ROWS + (row & (ROWS - 1)) >= b * KB + col)
                     p = jnp.where(seen, p, 0.0)
                 l_ref[r0:r1] += p[:, :128] + p[:, 128:]
-                o_ref[r0:r1] += jnp.dot(p.astype(bf16), v, preferred_element_type=f32)
+                o_ref[r0:r1] += mul(p.astype(bf16), v)
             return carry
 
         lax.fori_loop(0, 1024 // KB, block, 0)
-
-
-def attend(q, kv_all):
-    return pl.pallas_call(
-        attend_kernel,
-        out_shape=(
-            jax.ShapeDtypeStruct((NROW, HD), f32),
-            jax.ShapeDtypeStruct((NROW, HD), f32),
-        ),
-        in_specs=[VM, VM],
-        out_specs=(VM, VM),
-        compiler_params=params(),
-        name="attend",
-    )(q, kv_all)
 
 
 def attend_back_kernel(q_ref, do_ref, lse_ref, delta_ref, kv_ref, dq_ref, dkv_ref):
@@ -792,73 +964,32 @@
     w_gate, w_up, w_down, cotangent,
 ):
     s = (lax.axis_index("x") * 2 + lax.axis_index("c")) * 2 + lax.axis_index("t")
-    state = tokens.astype(f32)
-    normal_one, inverse_one = norm_forward(state)
-    normalized_input = (normal_one * norm_gain).astype(bf16)
-    stage = jnp.concatenate(
-        [
-            w.reshape(32, 4, -1)
-            for w in (w_query, key_matrix, value_matrix, w_out, w_gate, w_up, w_down)
-        ],
-        axis=2,
-    ).transpose(1, 0, 2)
-    normed_all, qkv, rest = spread(normalized_input, stage)
-    normed_all = normed_all.reshape(TOK, D)
-    qkv = qkv.reshape(D, QKV)
-    out_w = gather_weight(rest[:, :, :QC])
-    gate_up_w = gather_weight(rest[:, :, QC : QC + 2 * FC])
-    down_w = gather_weight(rest[:, :, QC + 2 * FC :])
-
-    projected = jnp.dot(normed_all, qkv, preferred_element_type=f32)
-    query_pre = projected[:, :QC].reshape(TOK, 2, HD)
-    key_pre = projected[:, QC : QC + KC].reshape(TOK, 1, HD)
-    value_bf = projected[:, QC + KC :].astype(bf16)
     at = jnp.arange(TOK, dtype=jnp.int32)
     position = (at // ROWS) * (NT * ROWS) + s * ROWS + at % ROWS
     exponent = jnp.arange(0, HD, 2, dtype=f32) / HD
     angles = position.astype(f32)[:, None] * (1.0 / rope_base**exponent)[None, :]
-    cosine, sine_table = jnp.cos(angles)[:, None, :], jnp.sin(angles)[:, None, :]
+    cosine, sine = jnp.cos(angles), jnp.sin(angles)
+    (
+        middle, grad_middle, gain_two, query_rows, grad_rows, lse2, delta, qk_pre, context_bf, part_two,
+        grad_middle_all, kv_all, qkv, normed_all, ffn_partial,
+    ) = forward(
+        tokens, cotangent, norm_gain.reshape(1, D), ffn_gain.reshape(1, D), query_gain.reshape(1, HD),
+        key_gain.reshape(1, HD), jnp.concatenate([cosine, cosine], axis=1),
+        jnp.concatenate([-sine, sine], axis=1),
+        w_query, key_matrix, value_matrix, w_out, w_gate, w_up, w_down,
+    )
+    state = tokens.astype(f32)
+    normal_one, inverse_one = norm_forward(state)
+    cosine, sine_table = cosine[:, None, :], sine[:, None, :]
+    normed_all = normed_all.reshape(TOK, D)
+    grad_middle_all = grad_middle_all.reshape(TOK, D)
+    qkv = qkv.reshape(D, QKV)
+    kv_all = kv_all.reshape(SEQ, 2 * KC)
+    query_pre = qk_pre[:, :QC].reshape(TOK, 2, HD)
+    key_pre = qk_pre[:, QC : QC + KC].reshape(TOK, 1, HD)
     query_normal, query_inverse = norm_forward(query_pre)
     key_normal, key_inverse = norm_forward(key_pre)
-    query_rot = rotate(query_normal * query_gain, cosine, sine_table).astype(bf16)
-    key_rot = rotate(key_normal * key_gain, cosine, sine_table).astype(bf16)
-    packed = jnp.concatenate([key_rot.reshape(TOK, KC), value_bf], axis=1)
-    kv_all, grad_all = gather_keys(packed, cotangent, 1)
-    query_rows = to_rows(query_rot)
-    raw, sums = attend(query_rows, kv_all)
-    total = jnp.sum(sums, axis=1, keepdims=True)
-    attended_rows = raw / total
-    lse2 = jnp.log2(total).reshape(1, NROW)
-    context_bf = from_rows(attended_rows).astype(bf16)
-    middle_state = state + sum_rows(cross_rows(context_bf, out_w), 2)
-    normal_two, inverse_two = norm_forward(middle_state)
-    normed_two = (normal_two * ffn_gain).astype(bf16)
-    normed_two_all = gather_rows(normed_two, 3)
-    gate_up = jnp.dot(normed_two_all, gate_up_w, preferred_element_type=f32)
-    gate_value = gate_up[:, :FC]
-    upward = gate_up[:, FC:]
-    sigmoid_gate = jax.nn.sigmoid(gate_value)
-    activated = gate_value * sigmoid_gate
-    hidden = (activated * upward).astype(bf16)
-    grad_hidden = jnp.dot(grad_all, down_w, preferred_element_type=f32)
-    grad_gate = grad_hidden * upward * (sigmoid_gate * (1.0 + gate_value * (1.0 - sigmoid_gate)))
-    grad_upward = grad_hidden * activated
-    grad_gate_up = jnp.concatenate([grad_gate, grad_upward], axis=1).astype(bf16)
-    grad_normed_two = sum_rows(cross_rows(grad_gate_up, gate_up_w), 4)
-    result = (middle_state + sum_rows(cross_rows(hidden, down_w), 5)).astype(bf16)
-    ffn_grads = scatter_weight(
-        jnp.concatenate(
-            [over_tokens(normed_two_all, grad_gate_up), over_tokens(grad_all, hidden)], axis=1
-        )
-    )
-    grad_middle = cotangent.astype(f32) + norm_backward(
-        grad_normed_two, normal_two, inverse_two, ffn_gain
-    )
-    gain_two = jnp.sum(grad_normed_two * normal_two, axis=0)
-    grad_middle_all = gather_rows(grad_middle.astype(bf16), 6)
-    grad_context = jnp.dot(grad_middle_all, out_w, preferred_element_type=f32).astype(bf16)
-    grad_rows = to_rows(grad_context)
-    delta = jnp.sum(grad_rows.astype(f32) * attended_rows, axis=1).reshape(1, NROW)
+    ffn_grads = scatter_weight(ffn_partial.reshape(D, PARTIAL))
     grad_query_rows, grad_packed = attend_back(query_rows, grad_rows, lse2, delta, kv_all)
     grad_own = sum_keys(grad_packed, 7)
     grad_key_rot = grad_own[:, :KC].reshape(TOK, 1, HD)
@@ -876,6 +1007,7 @@
         [grad_query_pre.astype(bf16), grad_key_pre.astype(bf16), grad_value_bf], axis=1
     )
     grad_normed = sum_rows(cross_rows(grad_projected, qkv), 8)
+    result = (middle + sum_rows(part_two.reshape(TOK, D), 5)).astype(bf16)
     grad_input = grad_middle + norm_backward(grad_normed, normal_one, inverse_one, norm_gain)
     gain_one = jnp.sum(grad_normed * normal_one, axis=0)
     attn_grads = scatter_weight(
@@ -890,7 +1022,7 @@
         cuts.append(cuts[-1] + w)
     grads = [back[:, :, a:b].reshape(32, -1) for a, b in zip(cuts[:-1], cuts[1:])]
     gain_one, gain_two, gain_query, gain_key = lax.psum(
-        (gain_one, gain_two, gain_query, gain_key), AXES
+        (gain_one, gain_two[0], gain_query, gain_key), AXES
     )
     return (
         result, grad_input, gain_one, grads[0], grads[1], grads[2], gain_query, gain_key, grads[3],

time: 630 us -> 541 us (0.86); the launches traced: 619 us -> 537 us
  matrix products: 53.3 us -> 4.74 us
  local copies, waits for them, and re-layouts: 43 us -> 14.9 us
  other arithmetic: 37.2 us -> 13.3 us
  Pallas kernels: 338 us -> 355 us
    pallas_call x5 -> x1, Pallas kernels: 138 us -> 202 us  [forward(): pl.pallas_call(forward_kernel, out_shape=(out((ROWS, D), f32), out((ROWS,...]
    pallas_call x4 -> x2, Pallas kernels: 95.6 us -> 46.7 us  [sum_rows(): pl.pallas_call(sum_kernel, out_shape=jax.ShapeDtypeStruct((ROWS, D), f32)...]
    reduce_scatter x2, waiting for transfers between devices: 21.3 us -> 62.8 us  [scatter_weight(): lax.psum_scatter(w.reshape(NW, NT * 16, -1), T_AXES, scatter_dimension=1,...]
    all_gather x3 -> x0, waiting for transfers between devices: 36.6 us -> none  [gather_weight(): return lax.all_gather(w, T_AXES, axis=1, tiled=True).reshape(D, w.shape[-1])]
    dot_general x4 -> x0, matrix products: 22 us -> none  [the longest x1 8.59 us: local(): gate_up = jnp.dot(normed_two_all, gate_up_w, preferred_element_type=f32)]
    dot_general x4 -> x1, matrix products: 17.3 us -> 2.65 us  [cross_rows(): lax.dot_general(left_side, right_side, (((1,), (1,)), ((), ())), preferre...]
    concatenate x5 -> x0, local copies, waits for them, and re-layouts: 13.4 us -> none  [the longest x1 12.7 us: local(): jnp.concatenate([over_tokens(normed_two_all, grad_gate_up), over_tokens(g...]
    dot_general x4 -> x2, matrix products: 14 us -> 2.09 us  [over_tokens(): lax.dot_general(left_side, right_side, (((0,), (0,)), ((), ())), preferre...]
  transfers between devices with their start and end apart: 5 -> 2, of which waited for: 2 -> 1; matrix products, arithmetic and copies ran while one was open for 12% -> 1% of each run, Pallas kernels for 24% -> 9%
where the time goes in v2:
time: 541 us; the launch traced here: 537 us
  Pallas kernels  355 us (66%)
  blocking collectives  71 us (13%)
  waiting for transfers between devices  63.3 us (12%)
  local copies, waits for them, and re-layouts  14.9 us (3%)
  between operations  14.7 us (3%)
  other arithmetic  13.3 us (2%)
    pallas_call x1, Pallas kernels, forward(): pl.pallas_call(forward_kernel, out_shape=(out((ROWS, D), f32), out((ROWS,...  202 us
    psum x1, blocking collectives, local(): lax.psum((gain_one, gain_two[0], gain_query, gain_key), AXES)  71 us
    reduce_scatter x2, waiting for transfers between devices, scatter_weight(): lax.psum_scatter(w.reshape(NW, NT * 16, -1), T_AXES, scatter_dimension=1,...  62.8 us
    pallas_call x2, Pallas kernels, sum_rows(): pl.pallas_call(sum_kernel, out_shape=jax.ShapeDtypeStruct((ROWS, D), f32)...  46.7 us
    pallas_call x1, Pallas kernels, sum_keys(): pl.pallas_call(sum_keys_kernel, out_shape=jax.ShapeDtypeStruct((NW, ROWS,...  43.9 us
    pallas_call x1, Pallas kernels, attend_back(): pl.pallas_call(attend_back_kernel, out_shape=(jax.ShapeDtypeStruct((NROW,...  32.4 us
    pallas_call x1, Pallas kernels, return_weights(): pl.pallas_call(return_kernel, out_shape=jax.ShapeDtypeStruct((4, 2, 16, c...  30.1 us
  transfers between devices with their start and end apart: 2, of which 1 were waited for; matrix products, arithmetic and copies ran while one was open for 1% of the time, Pallas kernels for 9%

profile of v2, /device:TPU:17, one launch (start us, length us, event | category | flops | bytes accessed | tf_op | source)
XLA Modules:
  0.0 537.5 jit_solution(7387584131237380375)
XLA Ops:
  7.9 1.0 fusion.25
  8.9 1.0 pad_maximum_fusion.4
  9.9 202.1 %forward.1 = (f32[64,2048]{1,0:T(8,128)}, f32[64,2048]{1,0:T(8,128)}, f32[1,2048]{1,0:T(1,128)}, bf16[1024,128]{1,0:T(8,128)(2,1)}, bf16[1024,128]{1,0:T(8,128)(...) custom-call(bf16[64,2048]{1,0:T(8,128)(2,1)} %tok.1, ...), custom_call_target="tpu_custom_call" | custom-call | tf_op jit(solution)/shard_map/forward/pallas_call | solution.py:665
  212.0 1.1 multiply_reduce_fusion.3
  213.1 1.1 fusion.39
  214.2 32.4 %attend_back.1 = (f32[1024,128]{1,0:T(8,128)}, bf16[8192,256]{1,0:T(8,128)(2,1)}) custom-call(bf16[1024,128]{1,0:T(8,128)(2,1)} %get-tuple-element.34.q_ref, bf16[1024,128]{1,0:T(8,128)(2,1)} %get-tuple-element.35.do_ref, f32[1,1024]{1,0:T(1,128)} %get-tuple-element.36.lse_ref, f32[1,1024]{1,0:T(1,128)} %get-tuple-element.37.delta_ref, ...), custom_call_target="tpu_custom_call" | custom-call | tf_op jit(solution)/shard_map/attend_back/pallas_call | solution.py:898
  246.6 43.9 %sum_keys.1 = f32[8,64,256]{2,1,0:T(8,128)} custom-call(bf16[8,4,2,2,64,256]{5,4,3,2,1,0:T(8,128)(2,1)} %bitcast.98), custom_call_target="tpu_custom_call" | custom-call | tf_op jit(solution)/shard_map/sum_keys/pallas_call | solution.py:752
  290.5 1.7 slice.102
  292.2 1.0 slice_bitcast_fusion.3
  295.8 1.2 fusion.18
  300.1 1.3 convolution_convert_fusion
  301.7 2.8 copy.96
  305.3 19.9 %sum_rows.2 = f32[64,2048]{1,0:T(8,128)} custom-call(bf16[8,64,2048]{2,1,0:T(8,128)(2,1)} %get-tuple-element.31.x_ref), custom_call_target="tpu_custom_call" | custom-call | tf_op jit(solution)/shard_map/sum_rows/pallas_call | solution.py:702
  325.2 2.7 convolution_convert_fusion.1
  327.9 26.8 %sum_rows.3 = f32[64,2048]{1,0:T(8,128)} custom-call(bf16[8,64,2048]{2,1,0:T(8,128)(2,1)} %bitcast.99), custom_call_target="tpu_custom_call" | custom-call | tf_op jit(solution)/shard_map/sum_rows/pallas_call | solution.py:702
  354.9 1.3 fusion.7
  356.3 71.0 %all-reduce = (f32[2048]{0:T(1024)}, f32[128]{0:T(128)}, f32[128]{0:T(128)}, f32[2048]{0:T(1024)}) all-reduce(f32[2048]{0:T(1024)S(1)} %get-tuple-element.49, f32[128]{0:T(128)S(1)} %bitcast_reduce_fusion, f32[128]{0:T(128)S(1)} %get-tuple-element.47, ...), channel_id=1, replica_groups=mesh['z'=4,'yl'=2,'x'=4,'c'=2,'t'=2] {'z','yl','x','c','t'}, use_global_device_ids=true, to_apply=%region_7.8 | all-reduce | flops 4352 | bytes 34816 | tf_op jit(solution)/shard_map/psum | solution.py:1024
  428.0 1.0 fusion.6
  429.0 62.8 %reduce-scatter.5.cloned.1.call-done = bf16[8,16,2304]{2,1,0:T(8,128)(2,1)} async-done(((bf16[8,256,2304]{2,1,0:T(8,128)(2,1)}), bf16[8,16,2304]{2,1,0:T(8,128)(2,1)}) %reduce-scatter.5.cloned.1.call-update) | async-done | bytes 589840 | tf_op jit(solution)/shard_map/reduce_scatter | solution.py:959
  491.9 2.0 pad_maximum_fusion.1.x_ref
  493.9 30.1 %return_weights.1 = bf16[4,2,16,3072]{3,2,1,0:T(8,128)(2,1)} custom-call(bf16[8,16,3072]{2,1,0:T(8,128)(2,1)} %pad_maximum_fusion.1.x_ref), custom_call_target="tpu_custom_call" | custom-call | tf_op jit(solution)/shard_map/return_weights/pallas_call | solution.py:824
  524.0 1.3 convert_bitcast_fusion
  526.7 0.8 copy.113
  528.8 0.8 copy.112
  (75 shorter events, 11.7 us)
Async XLA Ops:
  7.2 421.8 %reduce-scatter.3.cloned.1.call-start = ((), (), s32[]{:S(2)}) async-start(), calls=%async_computation.2 | async-start | bytes 3342336 | tf_op jit(solution)/shard_map/reduce_scatter | solution.py:959
  290.5 3.9 copy-start.6
  294.4 0.7 copy-start.12
  294.8 2.2 copy-start.1
  294.8 2.2 copy-start.11
  295.1 2.5 copy-start.16
  295.8 1.9 copy-start.15
  298.4 1.4 copy-start.7
  298.4 1.7 copy-start.14
  304.5 187.3 %reduce-scatter.5.cloned.1.call-start = ((), (), s32[]{:S(2)}) async-start(), calls=%async_computation.3 | async-start | bytes 10027008 | tf_op jit(solution)/shard_map/reduce_scatter | solution.py:959
  305.3 19.9 %copy-start.8 = (bf16[512,128]{1,0:T(8,128)(2,1)S(1)}, bf16[512,128]{1,0:T(8,128)(2,1)}, u32[]{:S(2)}) copy-start(bf16[512,128]{1,0:T(8,128)(2,1)} %slice.102) | copy-start | bytes 393220
  305.3 19.9 %copy-start.13 = (bf16[8,16,16,512]{3,2,1,0:T(8,128)(2,1)S(1)}, bf16[8,16,16,512]{3,2,1,0:T(8,128)(2,1)}, u32[]{:S(2)}) copy-start(bf16[8,16,16,512]{3,2,1,0:T(8,128)(2,1)} %get-tuple-element.41) | copy-start | bytes 6291460
  327.8 26.9 %copy-start.2 = (bf16[64,2048]{1,0:T(8,128)(2,1)S(1)}, bf16[64,2048]{1,0:T(8,128)(2,1)}, u32[]{:S(2)}) copy-start(bf16[64,2048]{1,0:T(8,128)(2,1)} %tok.1) | copy-start | bytes 786436
  327.9 27.0 %copy-start.9 = (f32[2048]{0:T(1024)S(1)}, f32[2048]{0:T(1024)}, u32[]{:S(2)}) copy-start(f32[2048]{0:T(1024)} %param.14) | copy-start | bytes 24580
  327.9 28.4 %copy-start.10 = (f32[1,2048]{1,0:T(1,128)S(1)}, f32[1,2048]{1,0:T(1,128)}, u32[]{:S(2)}) copy-start(f32[1,2048]{1,0:T(1,128)} %get-tuple-element.46) | copy-start | bytes 24580
  327.9 99.4 %copy-start.3 = (f32[64,2048]{1,0:T(8,128)S(1)}, f32[64,2048]{1,0:T(8,128)}, u32[]{:S(2)}) copy-start(f32[64,2048]{1,0:T(8,128)} %sum_rows.2) | copy-start | bytes 1572868
  327.9 99.4 %copy-start.5 = (f32[64,2048]{1,0:T(8,128)S(1)}, f32[64,2048]{1,0:T(8,128)}, u32[]{:S(2)}) copy-start(f32[64,2048]{1,0:T(8,128)} %get-tuple-element.30) | copy-start | bytes 1572868
  327.9 100.2 %copy-start.4 = (f32[64,2048]{1,0:T(8,128)S(1)}, f32[64,2048]{1,0:T(8,128)}, u32[]{:S(2)}) copy-start(f32[64,2048]{1,0:T(8,128)} %get-tuple-element.32) | copy-start | bytes 1572868
  354.7 73.3 %copy-start = (f32[64,2048]{1,0:T(8,128)S(1)}, f32[64,2048]{1,0:T(8,128)}, u32[]{:S(2)}) copy-start(f32[64,2048]{1,0:T(8,128)} %sum_rows.3) | copy-start | bytes 1572868
Sparse Core Ops, SparseCore 0:
  304.6 76.9 reduce-scatter.2
  386.0 105.7 reduce-scatter.4

commit v3 on v2

--- a/solution.py
+++ b/solution.py
@@ -687,149 +687,369 @@
     )(tok, cot, ngain, fgain, qgain, kgain, cosr, sinr, *weights)
 
 
-def sum_kernel(x_ref, out, part, land, ssem, rsem, local):
+class SumT:
+    KINDS = 9
+
+    def __init__(self, me, src, own, part, half, land, final, sends):
+        self.src, self.own, self.part, self.half, self.land, self.final, self.s = (
+            src, own, part, half, land, final, sends,
+        )
+        x = me["x"]
+        self.c, self.t = me["c"], me["t"]
+        self.order = (shifted(me, "x", 2), shifted(me, "x", 3), shifted(me, "x", 1), x)
+        self.dp, self.dm, self.dt, self.dc = t_devices(me)
+        self.h = part.shape[1] // 2
+
+    def leaf(self):
+        for i, xi in enumerate(self.order):
+            self.s.send(i, self.src.at[:, xi, 1 - self.c], self.part.at[i], self.dc)
+
+    def pair(self, i):
+        self.s.recv(i, self.part.at[i], self.dc)
+        mine = self.own(i, self.order[i])
+        self.part[i] = (self.part[i].astype(f32) + mine.astype(f32)).astype(bf16)
+
+    def two(self):
+        self.pair(0)
+        self.s.send(4, self.part.at[0, : self.h], self.half.at[0], self.dm)
+        self.s.send(5, self.part.at[0, self.h :], self.half.at[1], self.dp)
+        self.pair(1)
+        self.pair(2)
+
+    def three(self):
+        h = self.h
+        self.s.recv(4, self.half.at[0], self.dp)
+        self.part[1, :h] = (self.part[1, :h].astype(f32) + self.half[0].astype(f32)).astype(bf16)
+        self.s.send(6, self.part.at[1], self.land.at[0], self.dm)
+        self.s.recv(5, self.half.at[1], self.dm)
+        self.part[2, h:] = (self.part[2, h:].astype(f32) + self.half[1].astype(f32)).astype(bf16)
+        self.s.send(7, self.part.at[2], self.land.at[1], self.dp)
+        self.pair(3)
+
+    def four(self):
+        self.s.recv(6, self.land.at[0], self.dp)
+        self.s.recv(7, self.land.at[1], self.dm)
+        to = 1 - self.t
+        self.part[3, :, to] = (
+            self.part[3, :, to].astype(f32)
+            + self.land[0, :, to].astype(f32)
+            + self.land[1, :, to].astype(f32)
+        ).astype(bf16)
+        self.s.send(8, self.part.at[3, :, to], self.final, self.dt)
+
+    def total(self):
+        t = self.t
+        own = (
+            self.part[3, :, t].astype(f32)
+            + self.land[0, :, t].astype(f32)
+            + self.land[1, :, t].astype(f32)
+        )
+        self.s.recv(8, self.final, self.dt)
+        return own + self.final[...].astype(f32)
+
+
+def sum_t_scratch(slabs, rows, cols):
+    return [
+        pltpu.VMEM((4, slabs, 2, rows, cols), bf16),
+        pltpu.VMEM((2, slabs // 2, 2, rows, cols), bf16),
+        pltpu.VMEM((2, slabs, 2, rows, cols), bf16),
+        pltpu.VMEM((slabs, rows, cols), bf16),
+    ]
+
+
+class Return:
+    def __init__(self, me, x_ref, out, lo, hi, ssem, rsem, base, lsem):
+        self.x, self.out, self.lo, self.hi = x_ref, out, lo, hi
+        self.ssem, self.rsem, self.base, self.lsem = ssem, rsem, base, lsem
+        self.z, self.y, self.t = me["z"], me["yl"], me["t"]
+        self.own_g = 2 * self.z + self.y
+        self.holder = self.own_g // 4
+        self.block = self.own_g - 4 * self.holder
+        self.dy = w_devices(me)[2]
+
+    def each(self, act):
+        for g in range(8):
+            is_me = (self.own_g == g) & (self.holder == self.t)
+            act(g, is_me)
+
+    def start(self):
+        def act(g, is_me):
+            dst = self.out.at[self.block, self.t, :, self.lo : self.hi]
+            to = {"z": jnp.int32(g // 2), "yl": jnp.int32(g % 2), "t": self.holder}
+            k = self.base + self.block * 2 + self.t
+            c = remote(self.x.at[g], dst, self.ssem.at[self.base + g], self.rsem.at[k], to)
+            l = pltpu.make_async_copy(self.x.at[g], dst, self.lsem)
+
+            @pl.when(is_me)
+            def _():
+                l.start()
+                l.wait()
+
+            @pl.when(jnp.logical_not(is_me))
+            def _():
+                c.start()
+
+        self.each(act)
+
+    def end(self):
+        for j in range(4):
+            for t2 in range(2):
+                is_me = (2 * self.t + j // 2 == self.z) & (j % 2 == self.y) & (self.t == t2)
+
+                @pl.when(jnp.logical_not(is_me))
+                def _(j=j, t2=t2):
+                    d = self.out.at[j, t2, :, self.lo : self.hi]
+                    k = self.base + j * 2 + t2
+                    remote(d, d, self.ssem.at[0], self.rsem.at[k], self.dy).wait_recv()
+
+        def act(g, is_me):
+            @pl.when(jnp.logical_not(is_me))
+            def _():
+                x = self.x.at[g]
+                remote(x, x, self.ssem.at[self.base + g], self.rsem.at[0], self.dy).wait_send()
+
+        self.each(act)
+
+
+GAINS = 2 * D + 2 * HD
+PEERS_W = [(dz, dy) for dz in range(4) for dy in range(2) if dz or dy]
+PEERS_T = [(dx, dc, dt) for dx in range(4) for dc in range(2) for dt in range(2) if dx or dc or dt]
+BACKWARD_SEMS = 5 * SumT.KINDS + 2 * SUMW_SEMS + 3 * 8 + len(PEERS_W) + len(PEERS_T)
+
+
+def backward_kernel(
+    tok, middle, grad_mid, gain_two, ngain, qgain, kgain, cosr, sinr, q_rows, do_rows, lse, delta, qk_pre, ctx,
+    gm_in, part_two, kv_in, qkv_in, normed_in, partial,
+    result, grad_input, gains, back,
+    kv_all, wqkv, normed_all, gm_all, part_r, land_r, part, land, dq, dkv, gp, sa1, sa2, own_f,
+    ret_f, ret_1, ret_2, gsend, gw_land, gt_send, gt_land,
+    f1, f2, f3, f4, k11, k12, k13, k14, k21, k22, k23, k24, a11, a12, a13, a14, a21, a22, a23, a24,
+    ssem, rsem, lsem,
+):
     me = place()
-    barrier(w_devices(me))
-    c = pltpu.make_async_copy(x_ref, part, local)
-    c.start()
-    c.wait()
-    s = SumW(me, part, land, Sends(ssem, rsem))
-    out[...] = s.run()
-    s.s.close()
-
-
-def sum_rows(x, cid):
+    c = me["c"]
+    s = (me["x"] * 2 + c) * 2 + me["t"]
+    sem = pltpu.get_barrier_semaphore()
+    peers = [
+        {"z": shifted(me, "z", dz), "yl": shifted(me, "yl", dy), "t": shifted(me, "t", dt)}
+        for dz in range(4) for dy in range(2) for dt in range(2) if dz or dy or dt
+    ] + [
+        {"x": shifted(me, "x", dx), "c": shifted(me, "c", dc), "t": shifted(me, "t", dt)}
+        for dx in range(4) for dc in range(2) for dt in range(2) if dx or dc
+    ]
+    for d in peers:
+        pl.semaphore_signal(sem, inc=1, device_id=d, device_id_type=MESH)
+
+    count = [0]
+
+    def base(n):
+        count[0] += n
+        return count[0] - n
+
+    def sends(n):
+        return Sends(ssem, rsem, base(n))
+
+    sf = SumT(me, partial, lambda i, xi: own_f[i], f1, f2, f3, f4, sends(SumT.KINDS))
+    loads = [
+        pltpu.make_async_copy(part_two, part_r, lsem.at[0]),
+        pltpu.make_async_copy(kv_in, kv_all, lsem.at[1]),
+    ]
+    loads += [
+        pltpu.make_async_copy(partial.at[:, xi, c], own_f.at[i], lsem.at[2 + i])
+        for i, xi in enumerate(sf.order)
+    ]
+    loads += [
+        pltpu.make_async_copy(gm_in, gm_all, lsem.at[6]),
+        pltpu.make_async_copy(normed_in, normed_all, lsem.at[7]),
+        pltpu.make_async_copy(qkv_in, wqkv, lsem.at[8]),
+    ]
+    for l in loads:
+        l.start()
+    dq[...] = jnp.zeros_like(dq)
+    pl.semaphore_wait(sem, len(peers))
+
+    sf.leaf()
+    sr = SumW(me, part_r, land_r, sends(SUMW_SEMS))
+    loads[0].wait()
+    sr.leaf()
+    loads[1].wait()
+
+    def attention(slabs):
+        attend_back_blocks(slabs, s, q_rows, do_rows, lse, delta, kv_all, dq, dkv)
+
+    attention(range(0, 1))
+    sr.two()
+    for l in loads[2:]:
+        l.wait()
+    sf.two()
+    attention(range(1, 2))
+    sr.three()
+    attention(range(2, 3))
+    sf.three()
+    result[...] = (middle[...] + sr.total()).astype(bf16)
+    attention(range(3, 4))
+
+    def key_sum(lo, hi, bufs):
+        view = dkv.at[lo:hi]
+        return SumT(me, view, lambda i, xi: dkv[lo:hi, xi, c], *bufs, sends(SumT.KINDS))
+
+    k1 = key_sum(0, 4, (k11, k12, k13, k14))
+    k2 = key_sum(4, 8, (k21, k22, k23, k24))
+    k1.leaf()
+    sf.four()
+    attention(range(4, 6))
+    k1.two()
+    attention(range(6, 8))
+    k2.leaf()
+    k1.three()
+    ret_f[...] = sf.total().astype(bf16)
+    rf = Return(me, ret_f, back, QKV + QC, COLS, ssem, rsem, base(8), lsem.at[9])
+    rf.start()
+
+    for head in range(2):
+        u = qk_pre[:, head * HD : head * HD + HD]
+        g = dq[...].reshape(NW, 2, ROWS, HD)[:, head].reshape(TOK, HD) * score_scale
+        dpre, gain = head_back(u, g, qgain[...], cosr[...], sinr[...])
+        gp[:, head * HD : head * HD + HD] = dpre.astype(bf16)
+        gains[:, 2 * D : 2 * D + HD] = gain if head == 0 else gains[:, 2 * D : 2 * D + HD] + gain
+    k2.two()
+    k1.four()
+
+    def weight_step(dst, at, a_ref, lo, hi):
+        def step(g, carry):
+            a = a_ref[:, :, pl.ds(pl.multiple_of(g * 256, 256), 256)].reshape(TOK, 256)
+            b = ctx[...] if lo is None else gp[:, lo:hi]
+            dst[g, :, :, :, :, at : at + 256] = (
+                mul_tokens(a, b).astype(bf16).reshape(4, 2, 2, 16, 256)
+            )
+            return carry
+
+        lax.fori_loop(0, NW, step, 0)
+
+    weight_step(sa1, 0, gm_all, None, None)
+    k2.three()
+    weight_step(sa1, QC, normed_all, 0, QC)
+    a1 = SumT(me, sa1, lambda i, xi: sa1[:, xi, c], a11, a12, a13, a14, sends(SumT.KINDS))
+    a1.leaf()
+    k2.four()
+    a1.two()
+    own_kv = [k1.total().reshape(TOK // 2, 2 * KC), k2.total().reshape(TOK // 2, 2 * KC)]
+    for h in range(2):
+        rows = slice(h * 256, h * 256 + 256)
+        dpre, gain = head_back(
+            qk_pre[rows, QC:], own_kv[h][:, :KC], kgain[...], cosr[rows], sinr[rows]
+        )
+        gp[rows, QC : QC + KC] = dpre.astype(bf16)
+        gp[rows, QC + KC :] = own_kv[h][:, KC:].astype(bf16)
+        cols = slice(2 * D + HD, 2 * D + 2 * HD)
+        gains[:, cols] = gain if h == 0 else gains[:, cols] + gain
+    for n in range(4):
+        w = wqkv[2 * n : 2 * n + 2].reshape(512, QKV)
+        part[:, :, n * 512 : n * 512 + 512] = (
+            mul_rows(gp[...], w).astype(bf16).reshape(NW, ROWS, 512)
+        )
+    sw = SumW(me, part, land, sends(SUMW_SEMS))
+    sw.leaf()
+    weight_step(sa2, 0, normed_all, QC, QKV)
+    a2 = SumT(me, sa2, lambda i, xi: sa2[:, xi, c], a21, a22, a23, a24, sends(SumT.KINDS))
+    a2.leaf()
+    sw.two()
+    a1.three()
+    a2.two()
+    sw.three()
+    a1.four()
+    a2.three()
+    gnorm = sw.total()
+    x = tok[...].astype(f32)
+    inv = rms(x)
+    normal = x * inv
+    gains[:, :D] = jnp.sum(gnorm * normal, axis=0, keepdims=True)
+    gains[:, D : 2 * D] = gain_two[...]
+
+    bw = base(len(PEERS_W))
+    bt = base(len(PEERS_T))
+    gsend[...] = gains[...]
+    first = []
+    for i, (dz, dy) in enumerate(PEERS_W):
+        d = {"z": shifted(me, "z", dz), "yl": shifted(me, "yl", dy)}
+        first.append(remote(gsend, gw_land.at[i], ssem.at[bw + i], rsem.at[bw + i], d))
+        first[-1].start()
+    scaled = gnorm * ngain[...]
+    grad_input[...] = grad_mid[...] + inv * (
+        scaled - normal * jnp.mean(scaled * normal, axis=-1, keepdims=True)
+    )
+    ret_1[...] = a1.total().astype(bf16)
+    r1 = Return(me, ret_1, back, 0, 2 * QC, ssem, rsem, base(8), lsem.at[9])
+    r1.start()
+    a2.four()
+    total = gsend[...]
+    for i, r in enumerate(first):
+        r.wait_recv()
+        total = total + gw_land[i]
+    gt_send[...] = total
+    second = []
+    for i, (dx, dc, dt) in enumerate(PEERS_T):
+        d = {"x": shifted(me, "x", dx), "c": shifted(me, "c", dc), "t": shifted(me, "t", dt)}
+        second.append(remote(gt_send, gt_land.at[i], ssem.at[bt + i], rsem.at[bt + i], d))
+        second[-1].start()
+    ret_2[...] = a2.total().astype(bf16)
+    r2 = Return(me, ret_2, back, 2 * QC, 3 * QC, ssem, rsem, base(8), lsem.at[9])
+    r2.start()
+    for i, r in enumerate(second):
+        r.wait_recv()
+        total = total + gt_land[i]
+    gains[...] = total
+    for r in first + second:
+        r.wait_send()
+    for r in (rf, r1, r2):
+        r.end()
+    for g in (sf, sr, k1, k2, a1, a2, sw):
+        g.s.close()
+    assert count[0] == BACKWARD_SEMS, count[0]
+
+
+def head_back(u, g, gain, cosine, sine):
+    rolled = jnp.concatenate([g[:, HD // 2 :], g[:, : HD // 2]], axis=1)
+    g = g * cosine - rolled * sine
+    inv = rms(u)
+    normal = u * inv
+    total = jnp.sum(g * normal, axis=0, keepdims=True)
+    scaled = g * gain
+    return inv * (scaled - normal * jnp.mean(scaled * normal, axis=-1, keepdims=True)), total
+
+
+def backward(*args):
+    def out(shape, dtype):
+        return jax.ShapeDtypeStruct(shape, dtype)
+
+    def vmem(shape, dtype=bf16):
+        return pltpu.VMEM(shape, dtype)
+
     return pl.pallas_call(
-        sum_kernel,
-        out_shape=jax.ShapeDtypeStruct((ROWS, D), f32),
-        in_specs=[VM],
-        out_specs=VM,
-        scratch_shapes=[pltpu.VMEM((NW, ROWS, D), bf16), pltpu.VMEM((SUMW_ROWS, D), bf16)]
-        + sems(SUMW_SEMS) + [DMA(())],
-        compiler_params=params(cid),
-        name="sum_rows",
-    )(x.astype(bf16).reshape(NW, ROWS, D))
-
-
-def sum_keys_kernel(x_ref, out, part, half, land, final, ssem, rsem, local):
-    me = place()
-    barrier(t_devices(me))
-    x, c, t = me["x"], me["c"], me["t"]
-    xp, xm, xo = shifted(me, "x", 1), shifted(me, "x", 3), shifted(me, "x", 2)
-    dp, dm, dt, dc = t_devices(me)
-    s = Sends(ssem, rsem)
-    order = (xo, xm, xp, x)
-    for i, xi in enumerate(order):
-        s.send(i, x_ref.at[:, xi, 1 - c], part.at[i], dc)
-    for i, xi in enumerate(order):
-        s.recv(i, part.at[i], dc)
-        part[i] = (part[i].astype(f32) + x_ref[:, xi, c].astype(f32)).astype(bf16)
-        if i == 0:
-            s.send(4, part.at[0, 0:4], half.at[0], dm)
-            s.send(5, part.at[0, 4:8], half.at[1], dp)
-        if i == 1:
-            s.recv(4, half.at[0], dp)
-            part[1, 0:4] = (part[1, 0:4].astype(f32) + half[0].astype(f32)).astype(bf16)
-            s.send(6, part.at[1], land.at[0], dm)
-        if i == 2:
-            s.recv(5, half.at[1], dm)
-            part[2, 4:8] = (part[2, 4:8].astype(f32) + half[1].astype(f32)).astype(bf16)
-            s.send(7, part.at[2], land.at[1], dp)
-    s.recv(6, land.at[0], dp)
-    s.recv(7, land.at[1], dm)
-    to = 1 - t
-    part[3, :, to] = (
-        part[3, :, to].astype(f32) + land[0, :, to].astype(f32) + land[1, :, to].astype(f32)
-    ).astype(bf16)
-    s.send(8, part.at[3, :, to], final, dt)
-    own = part[3, :, t].astype(f32) + land[0, :, t].astype(f32) + land[1, :, t].astype(f32)
-    s.recv(8, final, dt)
-    out[...] = own + final[...].astype(f32)
-    s.close()
-
-
-def sum_keys(x, cid):
-    out = pl.pallas_call(
-        sum_keys_kernel,
-        out_shape=jax.ShapeDtypeStruct((NW, ROWS, 2 * KC), f32),
-        in_specs=[VM],
-        out_specs=VM,
+        backward_kernel,
+        out_shape=(
+            out((ROWS, D), bf16), out((ROWS, D), f32), out((1, GAINS), f32), out((4, 2, 16, COLS), bf16),
+        ),
+        in_specs=[VM] * 15 + [ANY] * 6,
+        out_specs=(VM,) * 4,
         scratch_shapes=[
-            pltpu.VMEM((4, NW, 2, ROWS, 2 * KC), bf16),
-            pltpu.VMEM((2, 4, 2, ROWS, 2 * KC), bf16),
-            pltpu.VMEM((2, NW, 2, ROWS, 2 * KC), bf16),
-            pltpu.VMEM((NW, ROWS, 2 * KC), bf16),
+            vmem((NW, NT, ROWS, 2 * KC)), vmem((NW, NT, 16, QKV)), vmem((NW, ROWS, D)), vmem((NW, ROWS, D)),
+            vmem((NW, ROWS, D)), vmem((SUMW_ROWS, D)), vmem((NW, ROWS, D)), vmem((SUMW_ROWS, D)),
+            vmem((NROW, HD), f32), vmem((NW, 4, 2, 2, ROWS, 2 * KC)), vmem((TOK, QKV)),
+            vmem((NW, 4, 2, 2, 16, 2 * QC)), vmem((NW, 4, 2, 2, 16, QC)), vmem((4, NW, 2, 16, PARTIAL)),
+            vmem((NW, 16, PARTIAL)), vmem((NW, 16, 2 * QC)), vmem((NW, 16, QC)),
+            vmem((1, GAINS), f32), vmem((len(PEERS_W), 1, GAINS), f32),
+            vmem((1, GAINS), f32), vmem((len(PEERS_T), 1, GAINS), f32),
         ]
-        + sems(9) + [DMA(())],
-        compiler_params=params(cid),
-        name="sum_keys",
-    )(x.reshape(NW, 4, 2, 2, ROWS, 2 * KC))
-    return out.reshape(TOK, 2 * KC)
-
-
-def return_kernel(x_ref, out, ssem, rsem, local):
-    me = place()
-    z, y, t = me["z"], me["yl"], me["t"]
-    own_g = 2 * z + y
-    sem = pltpu.get_barrier_semaphore()
-    for dz in range(4):
-        for dyl in range(2):
-            for dt in range(2):
-                if dz or dyl or dt:
-                    pl.semaphore_signal(
-                        sem, inc=1, device_id_type=MESH,
-                        device_id={
-                            "z": shifted(me, "z", dz), "yl": shifted(me, "yl", dyl), "t": shifted(me, "t", dt)
-                        },
-                    )
-    pl.semaphore_wait(sem, 15)
-    holder = own_g // 4
-    block = own_g - 4 * holder
-    for g in range(8):
-        is_me = (own_g == g) & (holder == t)
-        dst = out.at[block, t]
-        to = {"z": jnp.int32(g // 2), "yl": jnp.int32(g % 2), "t": holder}
-        c = remote(x_ref.at[g], dst, ssem.at[g], rsem.at[block * 2 + t], to)
-        l = pltpu.make_async_copy(x_ref.at[g], dst, local)
-
-        @pl.when(is_me)
-        def _():
-            l.start()
-            l.wait()
-
-        @pl.when(jnp.logical_not(is_me))
-        def _():
-            c.start()
-
-    dy = w_devices(me)[2]
-    for j in range(4):
-        for t2 in range(2):
-            is_me = (2 * t + j // 2 == z) & (j % 2 == y) & (t == t2)
-
-            @pl.when(jnp.logical_not(is_me))
-            def _(j=j, t2=t2):
-                d = out.at[j, t2]
-                remote(d, d, ssem.at[0], rsem.at[j * 2 + t2], dy).wait_recv()
-
-    for g in range(8):
-        is_me = (own_g == g) & (holder == t)
-
-        @pl.when(jnp.logical_not(is_me))
-        def _(g=g):
-            remote(x_ref.at[g], x_ref.at[g], ssem.at[g], rsem.at[0], dy).wait_send()
-
-
-def return_weights(x, cid):
-    cols = x.shape[-1]
-    return pl.pallas_call(
-        return_kernel,
-        out_shape=jax.ShapeDtypeStruct((4, 2, 16, cols), x.dtype),
-        in_specs=[VM],
-        out_specs=VM,
-        scratch_shapes=sems(8) + [DMA(())],
-        compiler_params=params(cid),
-        name="return_weights",
-    )(x)
+        + sum_t_scratch(NW, 16, PARTIAL)
+        + sum_t_scratch(4, ROWS, 2 * KC)
+        + sum_t_scratch(4, ROWS, 2 * KC)
+        + sum_t_scratch(NW, 16, 2 * QC)
+        + sum_t_scratch(NW, 16, QC)
+        + sems(BACKWARD_SEMS) + [DMA((10,))],
+        compiler_params=params(1),
+        name="backward",
+    )(*args)
 
 
 def attend_blocks(slabs, s, q_ref, kv_ref, o_ref, l_ref):
@@ -856,107 +1076,35 @@
         lax.fori_loop(0, 1024 // KB, block, 0)
 
 
-def attend_back_kernel(q_ref, do_ref, lse_ref, delta_ref, kv_ref, dq_ref, dkv_ref):
-    s = (lax.axis_index("x") * 2 + lax.axis_index("c")) * 2 + lax.axis_index("t")
-    dq_ref[...] = jnp.zeros_like(dq_ref)
+def attend_back_blocks(slabs, s, q_ref, do_ref, lse_ref, delta_ref, kv_ref, dq_ref, dkv_ref):
     factor = score_scale * LOG2E
-    for g in range(NW):
+    for g in slabs:
         first = g * CH
 
         def block(b, carry, g=g, first=first):
-            keys = pl.ds(pl.multiple_of(g * 1024 + b * KB, KB), KB)
-            k = kv_ref[keys, :KC]
-            v = kv_ref[keys, KC:]
+            pair = kv_ref[g, pl.ds(b * 4, 4)].reshape(KB, 2 * KC)
+            k, v = pair[:, :KC], pair[:, KC:]
             dk = jnp.zeros((KB, HD), f32)
             dv = jnp.zeros((KB, HD), f32)
             for r0 in range(first, NROW, 256):
                 r1 = min(r0 + 256, NROW)
                 q = q_ref[r0:r1]
                 do = do_ref[r0:r1]
-                sc = lax.dot_general(k, q, (((1,), (1,)), ((), ())), preferred_element_type=f32)
-                p = jnp.exp2(sc * factor - lse_ref[:, r0:r1])
+                p = jnp.exp2(mul_rows(k, q) * factor - lse_ref[:, r0:r1])
                 if r0 == first:
                     row = lax.broadcasted_iota(jnp.int32, (KB, r1 - r0), 1)
                     col = lax.broadcasted_iota(jnp.int32, (KB, r1 - r0), 0)
                     seen = (row >= CH) | (s * ROWS + (row & (ROWS - 1)) >= b * KB + col)
                     p = jnp.where(seen, p, 0.0)
-                dp = lax.dot_general(v, do, (((1,), (1,)), ((), ())), preferred_element_type=f32)
-                ds = (p * (dp - delta_ref[:, r0:r1])).astype(bf16)
-                dv = dv + jnp.dot(p.astype(bf16), do, preferred_element_type=f32)
-                dk = dk + jnp.dot(ds, q, preferred_element_type=f32)
-                dq_ref[r0:r1] += lax.dot_general(
-                    ds, k, (((0,), (0,)), ((), ())), preferred_element_type=f32
-                )
-            dkv_ref[keys, :KC] = (dk * score_scale).astype(bf16)
-            dkv_ref[keys, KC:] = dv.astype(bf16)
+                ds = (p * (mul_rows(v, do) - delta_ref[:, r0:r1])).astype(bf16)
+                dv = dv + mul(p.astype(bf16), do)
+                dk = dk + mul(ds, q)
+                dq_ref[r0:r1] += mul_tokens(ds, k)
+            both = jnp.concatenate([dk * score_scale, dv], axis=1).astype(bf16)
+            dkv_ref[g, b] = both.reshape(2, 2, ROWS, 2 * KC)
             return carry
 
         lax.fori_loop(0, 1024 // KB, block, 0)
-
-
-def attend_back(q, do, lse, delta, kv_all):
-    return pl.pallas_call(
-        attend_back_kernel,
-        out_shape=(
-            jax.ShapeDtypeStruct((NROW, HD), f32),
-            jax.ShapeDtypeStruct((SEQ, 2 * KC), bf16),
-        ),
-        in_specs=[VM] * 5,
-        out_specs=(VM, VM),
-        compiler_params=params(),
-        name="attend_back",
-    )(q, do, lse, delta, kv_all)
-
-
-def rotate(value_rows, cosine, sine_table):
-    middle = value_rows.shape[-1] // 2
-    first_half = value_rows[..., :middle]
-    second_half = value_rows[..., middle:]
-    return jnp.concatenate(
-        [
-            first_half * cosine - second_half * sine_table,
-            second_half * cosine + first_half * sine_table,
-        ],
-        axis=-1,
-    )
-
-
-def norm_forward(value_rows):
-    inverse = lax.rsqrt(jnp.mean(value_rows * value_rows, axis=-1, keepdims=True) + epsilon)
-    return (value_rows * inverse, inverse)
-
-
-def norm_backward(upstream, normal, inverse, gain):
-    scaled = upstream * gain
-    return inverse * (scaled - normal * jnp.mean(scaled * normal, axis=-1, keepdims=True))
-
-
-def cross_rows(left_side, right_side):
-    return lax.dot_general(
-        left_side, right_side, (((1,), (1,)), ((), ())), preferred_element_type=f32
-    )
-
-
-def over_tokens(left_side, right_side):
-    return lax.dot_general(
-        left_side, right_side, (((0,), (0,)), ((), ())), preferred_element_type=f32
-    ).astype(bf16)
-
-
-def to_rows(v):
-    return v.reshape(NW, ROWS, 2, HD).transpose(0, 2, 1, 3).reshape(NROW, HD)
-
-
-def from_rows(v):
-    return v.reshape(NW, 2, ROWS, HD).transpose(0, 2, 1, 3).reshape(TOK, 2 * HD)
-
-
-def gather_weight(w):
-    return lax.all_gather(w, T_AXES, axis=1, tiled=True).reshape(D, w.shape[-1])
-
-
-def scatter_weight(w):
-    return lax.psum_scatter(w.reshape(NW, NT * 16, -1), T_AXES, scatter_dimension=1, tiled=True)
 
 
 def local(
@@ -968,65 +1116,34 @@
     position = (at // ROWS) * (NT * ROWS) + s * ROWS + at % ROWS
     exponent = jnp.arange(0, HD, 2, dtype=f32) / HD
     angles = position.astype(f32)[:, None] * (1.0 / rope_base**exponent)[None, :]
-    cosine, sine = jnp.cos(angles), jnp.sin(angles)
+    cosine = jnp.cos(angles)
+    sine = jnp.sin(angles)
+    cosine = jnp.concatenate([cosine, cosine], axis=1)
+    sine = jnp.concatenate([-sine, sine], axis=1)
     (
         middle, grad_middle, gain_two, query_rows, grad_rows, lse2, delta, qk_pre, context_bf, part_two,
         grad_middle_all, kv_all, qkv, normed_all, ffn_partial,
     ) = forward(
         tokens, cotangent, norm_gain.reshape(1, D), ffn_gain.reshape(1, D), query_gain.reshape(1, HD),
-        key_gain.reshape(1, HD), jnp.concatenate([cosine, cosine], axis=1),
-        jnp.concatenate([-sine, sine], axis=1),
+        key_gain.reshape(1, HD), cosine, sine,
         w_query, key_matrix, value_matrix, w_out, w_gate, w_up, w_down,
     )
-    state = tokens.astype(f32)
-    normal_one, inverse_one = norm_forward(state)
-    cosine, sine_table = cosine[:, None, :], sine[:, None, :]
-    normed_all = normed_all.reshape(TOK, D)
-    grad_middle_all = grad_middle_all.reshape(TOK, D)
-    qkv = qkv.reshape(D, QKV)
-    kv_all = kv_all.reshape(SEQ, 2 * KC)
-    query_pre = qk_pre[:, :QC].reshape(TOK, 2, HD)
-    key_pre = qk_pre[:, QC : QC + KC].reshape(TOK, 1, HD)
-    query_normal, query_inverse = norm_forward(query_pre)
-    key_normal, key_inverse = norm_forward(key_pre)
-    ffn_grads = scatter_weight(ffn_partial.reshape(D, PARTIAL))
-    grad_query_rows, grad_packed = attend_back(query_rows, grad_rows, lse2, delta, kv_all)
-    grad_own = sum_keys(grad_packed, 7)
-    grad_key_rot = grad_own[:, :KC].reshape(TOK, 1, HD)
-    grad_value_bf = grad_own[:, KC:].astype(bf16)
-    grad_query_rot = from_rows(grad_query_rows * score_scale).reshape(TOK, 2, HD)
-    grad_query_norm = rotate(grad_query_rot, cosine, -sine_table)
-    grad_key_norm = rotate(grad_key_rot, cosine, -sine_table)
-    gain_query = jnp.sum(grad_query_norm * query_normal, axis=(0, 1))
-    gain_key = jnp.sum(grad_key_norm * key_normal, axis=(0, 1))
-    grad_query_pre = norm_backward(
-        grad_query_norm, query_normal, query_inverse, query_gain
-    ).reshape(TOK, QC)
-    grad_key_pre = norm_backward(grad_key_norm, key_normal, key_inverse, key_gain).reshape(TOK, KC)
-    grad_projected = jnp.concatenate(
-        [grad_query_pre.astype(bf16), grad_key_pre.astype(bf16), grad_value_bf], axis=1
+    result, grad_input, gains, back = backward(
+        tokens, middle, grad_middle, gain_two, norm_gain.reshape(1, D), query_gain.reshape(1, HD),
+        key_gain.reshape(1, HD), cosine, sine, query_rows, grad_rows, lse2, delta, qk_pre, context_bf,
+        grad_middle_all, part_two, kv_all, qkv, normed_all,
+        ffn_partial.reshape(NW, 4, 2, 2, 16, PARTIAL),
     )
-    grad_normed = sum_rows(cross_rows(grad_projected, qkv), 8)
-    result = (middle + sum_rows(part_two.reshape(TOK, D), 5)).astype(bf16)
-    grad_input = grad_middle + norm_backward(grad_normed, normal_one, inverse_one, norm_gain)
-    gain_one = jnp.sum(grad_normed * normal_one, axis=0)
-    attn_grads = scatter_weight(
-        jnp.concatenate(
-            [over_tokens(normed_all, grad_projected), over_tokens(grad_middle_all, context_bf)], axis=1
-        )
-    )
-    back = return_weights(jnp.concatenate([attn_grads, ffn_grads], axis=2), 9)
+    gains = gains[0]
     back = back.reshape(4, 32, COLS).transpose(1, 0, 2).astype(f32)
-    cuts = [0]
-    for w in (QC, KC, KC, QC, FC, FC, FC):
-        cuts.append(cuts[-1] + w)
-    grads = [back[:, :, a:b].reshape(32, -1) for a, b in zip(cuts[:-1], cuts[1:])]
-    gain_one, gain_two, gain_query, gain_key = lax.psum(
-        (gain_one, gain_two[0], gain_query, gain_key), AXES
-    )
+    grads, at = [], 0
+    for w in (QC, QC, KC, KC, FC, FC, FC):
+        grads.append(back[:, :, at : at + w].reshape(32, -1))
+        at += w
+    grad_out, grad_query, grad_key, grad_value, grad_gate, grad_up, grad_down = grads
     return (
-        result, grad_input, gain_one, grads[0], grads[1], grads[2], gain_query, gain_key, grads[3],
-        gain_two, grads[4], grads[5], grads[6],
+        result, grad_input, gains[:D], grad_query, grad_key, grad_value, gains[2 * D : 2 * D + HD],
+        gains[2 * D + HD :], grad_out, gains[D : 2 * D], grad_gate, grad_up, grad_down,
     )
 
 

time: 541 us -> 353 us (0.65)
  blocking collectives: 71 us -> 0 us
  waiting for transfers between devices: 63.3 us -> 0 us
  Pallas kernels: 355 us -> 333 us
  between operations: 14.7 us -> 1 us
  other arithmetic: 13.3 us -> 3.29 us
  local copies, waits for them, and re-layouts: 14.9 us -> 9.03 us
    psum x1 -> x0, blocking collectives: 71 us -> none  [local(): lax.psum((gain_one, gain_two[0], gain_query, gain_key), AXES)]
    reduce_scatter x2 -> x0, waiting for transfers between devices: 62.8 us -> none  [scatter_weight(): lax.psum_scatter(w.reshape(NW, NT * 16, -1), T_AXES, scatter_dimension=1,...]
    pallas_call x5 -> x1, Pallas kernels: 153 us -> 131 us  [backward(): pl.pallas_call(backward_kernel, out_shape=(out((ROWS, D), bf16), out((ROW...]
  transfers between devices with their start and end apart: 2 -> 0, of which waited for: 1 -> 0; matrix products, arithmetic and copies ran while one was open for 1% -> 0% of each run, Pallas kernels for 9% -> 0%
where the time goes in v3:
time: 353 us; the launch traced here: 347 us
  Pallas kernels  333 us (94%)
  local copies, waits for them, and re-layouts  9.03 us (3%)
    pallas_call x1, Pallas kernels, forward(): pl.pallas_call(forward_kernel, out_shape=(out((ROWS, D), f32), out((ROWS,...  202 us
    pallas_call x1, Pallas kernels, backward(): pl.pallas_call(backward_kernel, out_shape=(out((ROWS, D), bf16), out((ROW...  131 us

profile of v3, /device:TPU:17, one launch (start us, length us, event | category | flops | bytes accessed | tf_op | source)
XLA Modules:
  0.0 346.6 jit_solution(13306519486337844022)
XLA Ops:
  0.7 1.0 fusion
  1.7 1.0 pad_maximum_fusion
  2.7 202.1 %forward.1 = (f32[64,2048]{1,0:T(8,128)}, f32[64,2048]{1,0:T(8,128)}, f32[1,2048]{1,0:T(1,128)}, bf16[1024,128]{1,0:T(8,128)(2,1)}, bf16[1024,128]{1,0:T(8,128)(...) custom-call(bf16[64,2048]{1,0:T(8,128)(2,1)} %tok.3, ...), custom_call_target="tpu_custom_call" | custom-call | tf_op jit(solution)/shard_map/forward/pallas_call | solution.py:665
  204.7 131.3 %backward.1 = (bf16[64,2048]{1,0:T(8,128)(2,1)}, f32[64,2048]{1,0:T(8,128)}, f32[1,4352]{1,0:T(1,128)}, bf16[4,2,16,3072]{3,2,1,0:T(8,128)(2,1)}) custom-call(bf16[64,2048]{1,0:T(8,128)(2,1)} %tok.3, f32[64,2048]{1,0:T(8,128)} %get-tuple-element.32.middle, f32[64,2048]{1,0:T(8,128)} %get-tuple-element.33.grad_mid, f32[1,2048]{1,0:T(1,128)} %get-tuple-element.34.gain_two, ...), custom_call_target="tpu_custom_call" | custom-call | tf_op jit(solution)/shard_map/backward/pallas_call | solution.py:1028
  336.0 1.2 slice_bitcast_fusion.7
  337.2 1.3 fusion.12
  338.5 1.3 convert_bitcast_fusion
  339.8 0.6 copy.42
  340.5 0.6 copy.43
  341.1 0.0 copy-start.1
  341.1 0.1 slice_bitcast_fusion
  341.2 0.0 copy-start
  341.2 0.8 copy.39
  342.0 0.7 copy.36
  342.7 0.7 copy.33
  343.3 0.8 copy.38
  344.1 0.8 copy.37
  344.9 0.0 copy-done.1
  344.9 0.7 copy.46
  345.6 0.0 copy-done
  345.6 0.8 copy.47
  (4 shorter events, 0.1 us)
Async XLA Ops:
  341.1 3.8 %copy-start.1 = (bf16[64,2048]{1,0:T(8,128)(2,1)S(1)}, bf16[64,2048]{1,0:T(8,128)(2,1)}, u32[]{:S(2)}) copy-start(bf16[64,2048]{1,0:T(8,128)(2,1)} %get-tuple-element.80) | copy-start | bytes 786436
  341.2 4.4 %copy-start = (f32[64,2048]{1,0:T(8,128)S(1)}, f32[64,2048]{1,0:T(8,128)}, u32[]{:S(2)}) copy-start(f32[64,2048]{1,0:T(8,128)} %get-tuple-element.81) | copy-start | bytes 1572868
